TPU v7x, 32 devices: a whole 2x2x4 slice. The times are simulated.
32 devices in a mesh: img: 8 (over z, y), cls: 4 (over x, core).
Axes of the slice: x: 2, y: 2, z: 4, core: 2. Of those that a mesh axis runs over, the one named last changes fastest.
Arguments:
- embeddings: bfloat16 [768, 1024], P('img'), may hold values from -128 to 128
- class_text_embedding: bfloat16 [1024, 21888], P(None, 'cls'), may hold values from -1 to 1
- neighbours: int32 [768, 10], P('img'), may hold values from 0 to 223, as said below
- weights: float32 [768, 10], P('img'), may hold values from 0.2 to 1
- requests: int32 [8, 8, 16], P('img'), may hold values from -1 to 95, as said below
Outputs:
- labels: float32 [768, 21888], P('img', 'cls')
Inputs may be any that keep to these rules, and one draw needn't show every extreme that they name: requests[d, p, j] is a row index within device p's 96 rows, or -1 for an empty slot; the live slots of each (d, p) come first; requests[d, d] is empty; every d fills all 16 slots for one p. `neighbours`: a slot of 96 or more names a live request slot of the row's own device.
All inputs are finite; a program needn't handle non-finite values.
Results may differ from a plain program's by a relative error of at most 0.00085.
Values may be sent and summed in bfloat16 or wider, within the bound.
No kernel may reach another device: no remote copies, remote signals or barrier semaphores. Data moves between devices by JAX's collectives and lax.ppermute only.
A program may use at most 128 MiB of HBM per device.

v0:
```python
import functools
import jax
import jax.numpy as jnp
from jax import lax
from jax.experimental import pallas as pl
from jax.experimental.pallas import tpu as pltpu
from jax.sharding import PartitionSpec as P

LIVE = 21841
SMOOTHING = 1.0
TILE = 512
LANES = 128
CHUNK = 128
DEEP = 3
NT = (((1,), (1,)), ((), ()))
GROUP = 32
f32, bf16 = jnp.float32, jnp.bfloat16
VMEM = pltpu.VMEM
WHOLE = pl.BlockSpec(memory_space=VMEM)
SCALARS = pl.BlockSpec(memory_space=pltpu.SMEM)
ANYWHERE = pl.BlockSpec(memory_space=pl.ANY)
MIB = 2**20
FREE = pl.CostEstimate(flops=1000, bytes_accessed=1000, transcendentals=0)


def column_tiles(width):
    return [(a, min(a + TILE, width)) for a in range(0, width, TILE)]


def round_up(n, m):
    return -(-n // m) * m


def resident(x):
    return pltpu.with_memory_space_constraint(x, VMEM)


def exchange_plan(peers):
    direct = list(range(2, peers, 2))

    def cut(blocks):
        return [blocks[i : i + 4] for i in range(0, len(blocks), 4)]

    return direct + [1, 3], direct[1:], [[0]], cut(direct + [1]), cut([3] + [b ^ 1 for b in direct[1:]])


def streamed_from(width):
    tiles = column_tiles(width)
    return tiles[len(tiles) // 2][0]


def outside(x):
    return pltpu.with_memory_space_constraint(x, pltpu.HBM)


HBM = pl.BlockSpec(memory_space=pltpu.HBM)


def table_kernel(here_ref, requests_hbm, e_hbm, neighbours_hbm, weights_hbm, mine_ref, out_ref, table_ref, near_ref, weight_ref, requests_ref, sems):
    core, me = here_ref[1], here_ref[2]
    rows, depth = e_hbm.shape
    half = rows // 2
    peers, cap = requests_hbm.shape
    k = near_ref.shape[0]
    slots = round_up(k, 8)
    start = pl.multiple_of(core * half, 16)
    moves = (
        (requests_hbm, requests_ref),
        (neighbours_hbm, near_ref),
        (weights_hbm, weight_ref),
        (e_hbm.at[pl.ds(start, half), :], mine_ref.at[:, :depth]),
    )
    copies = [pltpu.make_async_copy(src, dst, sems.at[i]) for i, (src, dst) in enumerate(moves)]
    for copy in copies:
        copy.start()
    table_ref[...] = jnp.zeros_like(table_ref)
    for copy in copies[:3]:
        copy.wait()
    near = near_ref[...]
    slot = near - rows
    block = jnp.zeros_like(near) + me
    within = near
    for p in range(peers):
        block = jnp.where(slot >= p * cap, p, block)
        for j in range(cap):
            within = jnp.where(slot == p * cap + j, requests_ref[p, j], within)
    weight = weight_ref[...]
    w0 = weight.astype(bf16).astype(f32)
    w1 = (weight - w0).astype(bf16).astype(f32)
    w2 = weight - w0 - w1
    for i, x in enumerate((block.astype(f32), within.astype(f32), w0, w1, w2)):
        table_ref[i * slots : i * slots + k, :] = x
    out_ref[...] = table_ref[...].T.astype(bf16)
    mine_ref[:, depth:] = out_ref[pl.ds(start, half), :]
    copies[3].wait()


def tables_of(here, requests, embeddings, neighbours, weights):
    rows, depth = embeddings.shape
    k = neighbours.shape[1]
    return pl.pallas_call(
        table_kernel,
        in_specs=[SCALARS] + [HBM] * 4,
        out_specs=[WHOLE] * 2,
        out_shape=[VMEM((rows // 2, depth + LANES), bf16), VMEM((rows, LANES), bf16)],
        scratch_shapes=[
            VMEM((LANES, rows), f32),
            VMEM((k, rows), jnp.int32),
            VMEM((k, rows), f32),
            pltpu.SMEM(requests.shape, jnp.int32),
            pltpu.SemaphoreType.DMA((4,)),
        ],
        compiler_params=pltpu.CompilerParams(vmem_limit_bytes=MIB),
        cost_estimate=FREE,
        name="tables",
    )(here, outside(requests), outside(embeddings), outside(neighbours.T), outside(weights.T))


def split(x):
    hi = x.astype(bf16)
    return hi, (x - hi.astype(f32)).astype(bf16)


def dot(a, b):
    return jnp.dot(a, b, preferred_element_type=f32)


def powers_kernel(tiles, min_live, depth, first_row, n_parts, first, here_ref, *refs):
    parts, ct_ref = refs[:n_parts], refs[n_parts]
    if first:
        c_ref = refs[n_parts + 1]
        p_ref, tab_ref, top_ref, sum_ref, tile_ref, ct_ref, e_ref, sem = refs[-8:]
        split_at = streamed_from(c_ref.shape[0])
        load = pltpu.make_async_copy(c_ref.at[split_at:, :], ct_ref.at[split_at:, :], sem)
        load.start()
    else:
        p_ref, tab_ref, top_ref, sum_ref, tile_ref, e_ref = refs[-6:]
    core = here_ref[1]
    row = 0
    for i, part in enumerate(parts):
        n, at = part.shape[0], row
        if not first or i > 0:
            at = pl.multiple_of(row + n * (core if i % 2 == first else -core), 16)
        e_ref[pl.ds(at, n), :] = part[:, :depth]
        tab_ref[pl.ds(first_row + at, n), :] = part[:, depth:].astype(f32)
        row += n
    rows = slice(first_row, first_row + row)
    lane = lax.broadcasted_iota(jnp.int32, (row, LANES), 1)
    tops = jnp.full((row, LANES), -1e30, f32)
    sums = jnp.zeros((row, LANES), f32)
    for t, (a, b) in enumerate(tiles):
        if first and a == split_at:
            load.wait()
        logits = lax.dot_general(e_ref[...], ct_ref[a:b, :], NT, preferred_element_type=f32)
        if b > min_live:
            live = lax.broadcasted_iota(jnp.int32, logits.shape, 1) + a < here_ref[0]
            logits = jnp.where(live, logits, -1e30)
        top = jnp.max(logits, axis=1, keepdims=True)
        powers = jnp.exp(logits - top)
        if b > min_live:
            powers = jnp.where(live, powers, 0.0)
        p_ref[rows, a:b] = powers
        tops = jnp.where(lane == t, top, tops)
        sums = jnp.where(lane == t, jnp.sum(powers, axis=1, keepdims=True), sums)
    slots = tile_ref.shape[0]
    tops, sums = tops.T[:slots], sums.T[:slots]
    top = jnp.max(tops, axis=0, keepdims=True)
    tile_ref[...] = tops
    top_ref[...] = top
    sum_ref[...] = jnp.sum(sums * jnp.exp(tops - top), axis=0, keepdims=True)


def powers_of(parts, ct, classes, here, buffers, first_row, total_rows, min_live):
    first = buffers is None
    width, depth = ct.shape
    rows = sum(p.shape[0] for p in parts)
    tiles = column_tiles(width)
    slots = round_up(len(tiles), 8)
    n = len(parts)
    aliased = [] if first else list(buffers)
    out_shape = [
        VMEM((total_rows, width), f32),
        VMEM((total_rows, LANES), f32),
        VMEM((1, rows), f32),
        VMEM((1, rows), f32),
        VMEM((slots, rows), f32),
    ]
    scratch = [VMEM((rows, depth), bf16)]
    aliases = {2 + n + i: i for i in range(len(aliased))}
    if first:
        out_shape.append(VMEM((width, depth), bf16))
        scratch.append(pltpu.SemaphoreType.DMA)
        aliases = {1 + n: 5}
    return pl.pallas_call(
        functools.partial(powers_kernel, tiles, min_live, depth, first_row, n, first),
        in_specs=[SCALARS] + [WHOLE] * (n + 1) + ([HBM] if first else [WHOLE] * len(aliased)),
        out_specs=[WHOLE] * len(out_shape),
        out_shape=out_shape,
        scratch_shapes=scratch,
        input_output_aliases=aliases,
        compiler_params=pltpu.CompilerParams(vmem_limit_bytes=8 * MIB),
        cost_estimate=FREE,
        name="powers",
    )(here, *[resident(p) for p in parts], resident(ct), *([outside(classes)] if first else [resident(b) for b in aliased]))


def place_of(order, rows_here, me, block, within):
    relative = block ^ me
    place = jnp.zeros_like(block)
    for i, b in enumerate(order):
        place = jnp.where(relative == b, i * rows_here, place)
    return place + within


def prepare_kernel(order, total_rows, here_ref, table_ref, requests_hbm, near_hbm, weight_hbm, e_hbm, c_hbm, *refs):
    whi_ref, wlo_ref, scale_ref, asked_ref, pick_ref, own_ref, ct_ref, row_ref, near_ref, weight_ref, requests_ref, sems = refs
    me = here_ref[2]
    peers, cap = requests_hbm.shape
    k, rows_here = near_hbm.shape
    depth = e_hbm.shape[1]
    split_at = streamed_from(c_hbm.shape[0])
    moves = (
        (requests_hbm, requests_ref),
        (near_hbm, near_ref),
        (weight_hbm, weight_ref),
        (e_hbm, own_ref.at[:, :depth]),
        (c_hbm.at[:split_at, :], ct_ref.at[:split_at, :]),
    )
    copies = [pltpu.make_async_copy(src, dst, sems.at[i]) for i, (src, dst) in enumerate(moves)]
    for copy in copies:
        copy.start()
    own_ref[:, depth:] = table_ref[...]
    row_ref[...] = jnp.full_like(row_ref, -1)
    for copy in copies[:3]:
        copy.wait()
    lane = lax.broadcasted_iota(jnp.int32, (1, LANES), 1)
    for p in range(peers):
        start = place_of(order, rows_here, me, jnp.full((1, 1), p, jnp.int32), 0)
        row = jnp.full((1, LANES), -1, jnp.int32)
        for j in range(cap):
            row = jnp.where(lane == j, requests_ref[p, j], row)
        row_ref[p : p + 1, :] = jnp.where(row >= 0, row + start, -1)
    asked = row_ref[...].T
    column = lax.broadcasted_iota(jnp.int32, (cap, total_rows), 1)
    for p in range(peers):
        one = asked[:cap, p : p + 1]
        asked_ref[p * cap : (p + 1) * cap, :] = jnp.broadcast_to(one, (cap, LANES))
        pick_ref[p * cap : (p + 1) * cap, :] = jnp.where(column == one, 1.0, 0.0).astype(bf16)

    near, weight = near_ref[...].T, weight_ref[...].T
    column = lax.broadcasted_iota(jnp.int32, whi_ref.shape, 1)
    acc = jnp.zeros(whi_ref.shape, f32)
    for i in range(k):
        acc = acc + jnp.where(column == near[:, i : i + 1], SMOOTHING * weight[:, i : i + 1], 0.0)
    scale = 1.0 / (1.0 + SMOOTHING * jnp.sum(weight, axis=1, keepdims=True))
    whi_ref[...], wlo_ref[...] = split(acc * scale)
    scale_ref[...] = jnp.broadcast_to(scale, scale_ref.shape)
    for copy in copies[3:]:
        copy.wait()


def prepared(here, table, requests, neighbours, weights, embeddings, classes, order, total_rows):
    rows_here, depth = embeddings.shape
    width = classes.shape[0]
    k = neighbours.shape[1]
    extended = rows_here + requests.size
    return pl.pallas_call(
        functools.partial(prepare_kernel, order, total_rows),
        in_specs=[SCALARS, WHOLE] + [HBM] * 5,
        out_specs=[WHOLE] * 7,
        out_shape=[
            VMEM((rows_here, extended), bf16),
            VMEM((rows_here, extended), bf16),
            VMEM((rows_here, LANES), f32),
            VMEM((requests.size, LANES), jnp.int32),
            VMEM((requests.size, total_rows), bf16),
            VMEM((rows_here, depth + LANES), bf16),
            VMEM((width, depth), bf16),
        ],
        scratch_shapes=[
            VMEM((LANES, LANES), jnp.int32),
            VMEM((k, rows_here), jnp.int32),
            VMEM((k, rows_here), f32),
            pltpu.SMEM(requests.shape, jnp.int32),
            pltpu.SemaphoreType.DMA((5,)),
        ],
        compiler_params=pltpu.CompilerParams(vmem_limit_bytes=(2 if total_rows <= 768 else 8) * MIB),
        cost_estimate=FREE,
        name="prepare",
    )(here, resident(table), *[outside(x) for x in (requests, neighbours.T, weights.T, embeddings, classes)])


def graph_kernel(order, k, here_ref, whi_ref, wlo_ref, scale_ref, asked_ref, pick_ref, tab_ref, m_ref, rows_ref, thi_ref, tlo_ref):
    me = here_ref[2]
    total_rows = tab_ref.shape[0]
    rows_here, extended = whi_ref.shape
    slots = round_up(k, 8)
    rows_ref[:rows_here, :] = tab_ref[:rows_here, :]
    rows_ref[rows_here:, :] = dot(pick_ref[...], tab_ref[...].astype(bf16))
    column = lax.broadcasted_iota(jnp.int32, (GROUP, total_rows), 1)
    sub = lax.broadcasted_iota(jnp.int32, (GROUP, LANES), 0)
    for start in range(0, extended, GROUP):
        tab = rows_ref[start : start + GROUP, :]
        within = pltpu.roll(tab, LANES - slots, 1).astype(jnp.int32)
        weight = pltpu.roll(tab, LANES - 2 * slots, 1) + pltpu.roll(tab, LANES - 3 * slots, 1) + pltpu.roll(tab, LANES - 4 * slots, 1)
        place = place_of(order, rows_here, me, tab.astype(jnp.int32), within)
        itself = sub + start if start < rows_here else asked_ref[start - rows_here : start - rows_here + GROUP, :]
        acc = jnp.where(column == itself[:, :1], 1.0, 0.0)
        degree = jnp.zeros((GROUP, 1), f32)
        for i in range(k):
            w = weight[:, i : i + 1]
            acc = acc + jnp.where(column == place[:, i : i + 1], SMOOTHING * w, 0.0)
            degree = degree + w
        thi_ref[start : start + GROUP, :], tlo_ref[start : start + GROUP, :] = split(acc * (1.0 / (1.0 + SMOOTHING * degree)))
    column = lax.broadcasted_iota(jnp.int32, (rows_here, total_rows), 1)
    sub = lax.broadcasted_iota(jnp.int32, (rows_here, total_rows), 0)
    own = jnp.where(column == sub, scale_ref[:, :1], 0.0)
    thi = thi_ref[...]
    m_ref[...] = own + dot(whi_ref[...], thi) + dot(wlo_ref[...], thi) + dot(whi_ref[...], tlo_ref[...])


def graph_of(here, edges, tab, order, k):
    total_rows = tab.shape[0]
    rows_here, extended = edges[0].shape
    return pl.pallas_call(
        functools.partial(graph_kernel, order, k),
        in_specs=[SCALARS] + [WHOLE] * 6,
        out_specs=WHOLE,
        out_shape=VMEM((rows_here, total_rows), f32),
        scratch_shapes=[VMEM((extended, LANES), f32), VMEM((extended, total_rows), bf16), VMEM((extended, total_rows), bf16)],
        compiler_params=pltpu.CompilerParams(vmem_limit_bytes=(6 if total_rows <= 768 else 20) * MIB),
        cost_estimate=FREE,
        name="graph",
    )(here, *[resident(x) for x in edges], resident(tab))


def apply_kernel(tiles, n_pieces, n_cls, m_ref, p_ref, *refs):
    tile_refs, top_refs, sum_refs = refs[:n_pieces], refs[n_pieces : 2 * n_pieces], refs[2 * n_pieces : 3 * n_pieces]
    far_refs = refs[3 * n_pieces : 3 * n_pieces + n_cls - 1]
    out_ref, _, staged, sems = refs[3 * n_pieces + n_cls - 1 :]
    rows_here = m_ref.shape[0]

    def row(pieces):
        return jnp.concatenate([p[...] for p in pieces], axis=1)

    tops = [row(top_refs)] + [r[0:1, :] for r in far_refs]
    sums = [row(sum_refs)] + [r[1:2, :] for r in far_refs]
    top = functools.reduce(jnp.maximum, tops)
    total = sum(s * jnp.exp(t - top) for s, t in zip(sums, tops))
    factors = jnp.exp(row(tile_refs) - top) / total
    copies = []
    for t, (a, b) in enumerate(tiles):
        whi, wlo = split(m_ref[...] * factors[t : t + 1, :])
        hi, lo = split(p_ref[:, a:b])
        x = dot(jnp.concatenate([whi, wlo], axis=0), hi)
        staged[:, a:b] = x[:rows_here] + x[rows_here:] + dot(whi, lo)
        copy = pltpu.make_async_copy(staged.at[:, a:b], out_ref.at[:, a:b], sems.at[t])
        copy.start()
        copies.append(copy)
    for copy in copies:
        copy.wait()


def applied(m, powers, tile_tops, tops, sums, far):
    rows_here, total_rows = m.shape
    width = powers.shape[1]
    tiles = column_tiles(width)
    operands = [m, powers, *tile_tops, *tops, *sums, *far]
    return pl.pallas_call(
        functools.partial(apply_kernel, tiles, len(tops), len(far) + 1),
        in_specs=[WHOLE] * len(operands),
        out_specs=[ANYWHERE, WHOLE],
        out_shape=[jax.ShapeDtypeStruct((rows_here, width), f32), VMEM(powers.shape, f32)],
        input_output_aliases={1: 1},
        scratch_shapes=[VMEM((rows_here, width), f32), pltpu.SemaphoreType.DMA((len(tiles),))],
        compiler_params=pltpu.CompilerParams(vmem_limit_bytes=(8 if total_rows <= 768 else 16) * MIB),
        cost_estimate=FREE,
        name="smooth",
    )(*[resident(x) for x in operands])[0]


def shards(n_img, n_cls, embeddings, class_text_embedding, neighbours, weights, requests):
    rows_here = embeddings.shape[0]
    width = class_text_embedding.shape[1]
    half = rows_here // 2
    me, col = lax.axis_index("img"), lax.axis_index("cls")
    total_rows = n_img * rows_here
    here = jnp.stack([jnp.minimum(LIVE - col * width, width), col & 1, me]).astype(jnp.int32)
    min_live = min(width, LIVE - (n_cls - 1) * width)

    classes = class_text_embedding.T
    mine, table = tables_of(here, requests[0], embeddings, neighbours, weights)
    first, relayed, before, beside, last = exchange_plan(n_img)
    order = [b for piece in before + beside + last for b in piece]

    def swap(x):
        return lax.ppermute(x, "cls", [(i, i ^ 1) for i in range(n_cls)])

    def exchange(x, step):
        return lax.ppermute(x, "img", [(i, i ^ step) for i in range(n_img)])

    def halves(x, blocks):
        other = swap(x)
        cuts = [slice(i * half, (i + 1) * half) for i in range(len(blocks))]
        return {b: [x[c], other[c]] for b, c in zip(blocks, cuts)}

    *edges, own, ct = prepared(here, table, requests[0], neighbours, weights, embeddings, classes, order, total_rows)
    buffers, first_row, tops, sums, tile_tops = None, 0, [], [], []

    def work(blocks):
        nonlocal ct, buffers, first_row
        parts = [x for b in blocks for x in pairs[b]]
        results = powers_of(parts, ct, classes, here, buffers, first_row, total_rows, min_live)
        if buffers is None:
            ct = results[5]
        buffers = results[:2]
        first_row += len(blocks) * rows_here
        tops.append(results[2])
        sums.append(results[3])
        tile_tops.append(results[4])

    pairs = {0: [own]}
    for piece in before:
        work(piece)
    held = [exchange(mine, b) for b in first]
    *held, tops[-1] = lax.optimization_barrier((*held, tops[-1]))
    got = exchange(jnp.concatenate([x for b, x in zip(first, held) if b in relayed], axis=0), 1)
    pairs |= halves(jnp.concatenate(held, axis=0), first)
    for piece in beside:
        work(piece)
    got, tops[-1] = lax.optimization_barrier((got, tops[-1]))
    pairs |= halves(got, [b ^ 1 for b in relayed])
    for piece in last:
        work(piece)
    powers, tab = buffers
    stats = jnp.concatenate([jnp.concatenate(tops, axis=1), jnp.concatenate(sums, axis=1)], axis=0)
    far = [lax.ppermute(stats, "cls", [(i, i ^ d) for i in range(n_cls)]) for d in range(1, n_cls)]
    m = graph_of(here, edges, tab, order, neighbours.shape[1])
    return applied(m, powers, tile_tops, tops, sums, far)


def solution(mesh):
    in_specs = (
        P("img", None),
        P(None, "cls"),
        P("img", None),
        P("img", None),
        P("img", None, None),
    )
    sizes = mesh.shape
    run = functools.partial(shards, sizes["img"], sizes["cls"])
    return jax.shard_map(run, mesh=mesh, in_specs=in_specs, out_specs=P("img", "cls"), check_vma=False)
```

profile of v0, /device:TPU:0, one launch (start us, length us, event | category | flops | bytes accessed | tf_op | source)
XLA Modules:
  0.0 44.0 jit_solution(14541099079282376923)
XLA Ops:
  0.0 0.1 pad_add_fusion.here_ref
  0.1 1.5 %tables.1 = (bf16[48,1152]{1,0:T(8,128)(2,1)S(1)}, bf16[96,128]{1,0:T(8,128)(2,1)S(1)}) custom-call(s32[3]{0:T(128)S(1)} %pad_add_fusion.here_ref, s32[8,16]{1,0:T(8,128)} %bitcast.13, bf16[96,1024]{1,0:T(8,128)(2,1)} %e_hbm.3, s32[10,96]{1,0:T(8,128)} %bitcast.9, f32[10,96]{1,0:T(8,128)} %bitcast.11), custom_call_target="tpu_custom_call" | custom-call | flops 1000 | bytes 1000 | tf_op jit(solution)/shard_map/tables/pallas_call | solution.py:101
  1.6 3.1 %collective-permute-start = (bf16[48,1152]{1,0:T(8,128)(2,1)S(1)}, bf16[48,1152]{1,0:T(8,128)(2,1)S(1)}, u32[]{:S(2)}, u32[]{:S(2)}) collective-permute-start(bf16[48,1152]{1,0:T(8,128)(2,1)S(1)} %get-tuple-element.45), channel_id=1, source_target_pairs={{0,8},{4,12},{8,0},{12,4},{16,24},{20,28},{24,16},{28,20},{1,9},{5... | collective-permute-start | bytes 331784 | tf_op jit(solution)/shard_map/ppermute | solution.py:400
  4.7 2.6 %collective-permute-start.1 = (bf16[48,1152]{1,0:T(8,128)(2,1)S(1)}, bf16[48,1152]{1,0:T(8,128)(2,1)S(1)}, u32[]{:S(2)}, u32[]{:S(2)}) collective-permute-start(bf16[48,1152]{1,0:T(8,128)(2,1)S(1)} %get-tuple-element.45), channel_id=1, source_target_pairs={{0,16},{4,20},{8,24},{12,28},{16,0},{20,4},{24,8},{28,12},{1,17},{... | collective-permute-start | bytes 331784 | tf_op jit(solution)/shard_map/ppermute | solution.py:400
  7.3 0.0 collective-permute-start.2
  7.3 1.7 %collective-permute-start.3 = (bf16[48,1152]{1,0:T(8,128)(2,1)S(1)}, bf16[48,1152]{1,0:T(8,128)(2,1)S(1)}, u32[]{:S(2)}, u32[]{:S(2)}) collective-permute-start(bf16[48,1152]{1,0:T(8,128)(2,1)S(1)} %get-tuple-element.45), channel_id=1, source_target_pairs={{0,4},{4,0},{8,12},{12,8},{16,20},{20,16},{24,28},{28,24},{1,5},{5... | collective-permute-start | bytes 331784 | tf_op jit(solution)/shard_map/ppermute | solution.py:400
  9.0 0.6 %collective-permute-start.4 = (bf16[48,1152]{1,0:T(8,128)(2,1)S(1)}, bf16[48,1152]{1,0:T(8,128)(2,1)S(1)}, u32[]{:S(2)}, u32[]{:S(2)}) collective-permute-start(bf16[48,1152]{1,0:T(8,128)(2,1)S(1)} %get-tuple-element.45), channel_id=1, source_target_pairs={{0,12},{4,8},{8,4},{12,0},{16,28},{20,24},{24,20},{28,16},{1,13},{... | collective-permute-start | bytes 331784 | tf_op jit(solution)/shard_map/ppermute | solution.py:400
  9.6 3.2 %prepare.1 = (bf16[96,224]{1,0:T(8,128)(2,1)S(1)}, bf16[96,224]{1,0:T(8,128)(2,1)S(1)}, f32[96,128]{1,0:T(8,128)S(1)}, s32[128,128]{1,0:T(8,128)S(1)}, bf16[128,...) custom-call(s32[3]{0:T(128)S(1)} %pad_add_fusion.here_ref, ...), custom_call_target="tpu_custom_call" | custom-call | flops 1000 | bytes 1000 | tf_op jit(solution)/shard_map/prepare/pallas_call | solution.py:267
  12.9 5.5 %powers.3 = (f32[768,5472]{1,0:T(8,128)S(1)}, f32[768,128]{1,0:T(8,128)S(1)}, f32[1,96]{1,0:T(1,128)S(1)}, f32[1,96]{1,0:T(1,128)S(1)}, f32[16,96]{1,0:T(8,128)S(1)}, /*index=5*/bf16[5472,1024]{1,0:T(8,128)(2,1)S(1)}) custom-call(s32[3]{0:T(128)S(1)} %pad_add_fusion.here_ref, ...), custom_call_target="tpu_custom_call", output_to_operand_aliasing={{5}: (2, {})} | custom-call | flops 1000 | bytes 1000 | tf_op jit(solution)/shard_map/powers/pallas_call | solution.py:194
  18.4 0.0 collective-permute-done.refs_0_
  18.4 0.0 collective-permute-done.1.refs_2_
  18.4 0.0 collective-permute-done.2.refs_4_
  18.4 0.0 collective-permute-done.3.refs_6_
  18.4 0.0 collective-permute-done.4.refs_0_
  18.5 0.1 collective-permute-start.5
  18.6 1.6 %collective-permute-start.6 = (bf16[96,1152]{1,0:T(8,128)(2,1)S(1)}, bf16[96,1152]{1,0:T(8,128)(2,1)S(1)}, u32[]{:S(2)}, u32[]{:S(2)}) collective-permute-start(bf16[96,1152]{1,0:T(8,128)(2,1)S(1)} %pad_maximum_fusion), channel_id=1, source_target_pairs={{0,4},{4,0},{8,12},{12,8},{16,20},{20,16},{24,28},{28,24},{1,5},{5... | collective-permute-start | bytes 663560 | tf_op jit(solution)/shard_map/ppermute | solution.py:400
  20.2 0.3 collective-permute-done.5
  20.6 5.8 %powers.4 = (f32[768,5472]{1,0:T(8,128)S(1)}, f32[768,128]{1,0:T(8,128)S(1)}, f32[1,384]{1,0:T(1,128)S(1)}, f32[1,384]{1,0:T(1,128)S(1)}, f32[16,384]{1,0:T(8,128)S(1)}) custom-call(s32[3]{0:T(128)S(1)} %pad_add_fusion.here_ref, bf16[48,1152]{1,0:T(8,128)(2,1)S(1)} %collective-permute-done.refs_0_, ...), custom_call_target="tpu_custom_call", output_to_operand_aliasing={{0}: (10, {}), {1}: (11, {})} | custom-call | flops 1000 | bytes 1000 | tf_op jit(solution)/shard_map/powers/pallas_call | solution.py:194
  26.4 0.1 collective-permute-done.6
  26.5 0.1 collective-permute-start.7
  26.6 1.4 %collective-permute-done.7 = bf16[96,1152]{1,0:T(8,128)(2,1)S(1)} collective-permute-done((bf16[96,1152]{1,0:T(8,128)(2,1)S(1)}, bf16[96,1152]{1,0:T(8,128)(2,1)S(1)}, u32[]{:S(2)}, u32[]{:S(2)}) %collective-permute-start.7) | collective-permute-done | bytes 221216 | tf_op jit(solution)/shard_map/ppermute | solution.py:397
  28.0 4.6 %powers.5 = (f32[768,5472]{1,0:T(8,128)S(1)}, f32[768,128]{1,0:T(8,128)S(1)}, f32[1,288]{1,0:T(1,128)S(1)}, f32[1,288]{1,0:T(1,128)S(1)}, f32[16,288]{1,0:T(8,128)S(1)}) custom-call(s32[3]{0:T(128)S(1)} %pad_add_fusion.here_ref, bf16[48,1152]{1,0:T(8,128)(2,1)S(1)} %collective-permute-done.4.refs_0_, ...), custom_call_target="tpu_custom_call", output_to_operand_aliasing={{0}: (8, {}), {1}: (9, {})} | custom-call | flops 1000 | bytes 1000 | tf_op jit(solution)/shard_map/powers/pallas_call | solution.py:194
  32.6 0.1 maximum_maximum_fusion
  32.7 1.5 %collective-permute-start.10 = (f32[2,768]{1,0:T(2,128)S(1)}, f32[2,768]{1,0:T(2,128)S(1)}, u32[]{:S(2)}, u32[]{:S(2)}) collective-permute-start(f32[2,768]{1,0:T(2,128)S(1)} %maximum_maximum_fusion), channel_id=1, source_target_pairs={{0,3},{1,2},{2,1},{3,0},{4,7},{5,6},{6,5},{7,4},{8,11},{9,10},{10,... | collective-permute-start | bytes 18440 | tf_op jit(solution)/shard_map/ppermute | solution.py:437
  34.2 0.4 collective-permute-start.8
  34.5 0.5 %collective-permute-start.9 = (f32[2,768]{1,0:T(2,128)S(1)}, f32[2,768]{1,0:T(2,128)S(1)}, u32[]{:S(2)}, u32[]{:S(2)}) collective-permute-start(f32[2,768]{1,0:T(2,128)S(1)} %maximum_maximum_fusion), channel_id=1, source_target_pairs={{0,2},{1,3},{2,0},{3,1},{4,6},{5,7},{6,4},{7,5},{8,10},{9,11},{10,... | collective-permute-start | bytes 18440 | tf_op jit(solution)/shard_map/ppermute | solution.py:437
  35.1 3.8 %graph.1.m_ref = f32[96,768]{1,0:T(8,128)S(1)} custom-call(s32[3]{0:T(128)S(1)} %pad_add_fusion.here_ref, bf16[96,224]{1,0:T(8,128)(2,1)S(1)} %get-tuple-element.40.whi_ref, bf16[96,224]{1,0:T(8,128)(2,1)S(1)} %get-tuple-element.41.wlo_ref, f32[96,128]{1,0:T(8,128)S(1)} %get-tuple-element.42.scale_ref, s32[128,128]{1,0:T(8,128)S(1)} %get-tuple-element.43.asked_ref, ...), custom_call_target="tpu_custom_call" | custom-call | flops 1000 | bytes 1000 | tf_op jit(solution)/shard_map/graph/pallas_call | solution.py:325
  38.9 0.0 collective-permute-done.10.refs_11_
  38.9 0.0 collective-permute-done.8.refs_9_
  39.0 0.0 collective-permute-done.9.refs_10_
  39.0 4.8 %smooth.1 = (f32[96,5472]{1,0:T(8,128)}, f32[768,5472]{1,0:T(8,128)S(1)}) custom-call(f32[96,768]{1,0:T(8,128)S(1)} %graph.1.m_ref, f32[768,5472]{1,0:T(8,128)S(1)} %get-tuple-element.62.p_ref, f32[16,96]{1,0:T(8,128)S(1)} %get-tuple-element.63.refs_0_, f32[16,384]{1,0:T(8,128)S(1)} %get-tuple-element.64.refs_1_, ...), custom_call_target="tpu_custom_call", output_to_operand_aliasing={{1}: (1, {})} | custom-call | flops 1000 | bytes 1000 | tf_op jit(solution)/shard_map/smooth/pallas_call | solution.py:369
  (9 shorter events, 0.2 us)
Async XLA Ops:
  1.6 16.8 %collective-permute-start = (bf16[48,1152]{1,0:T(8,128)(2,1)S(1)}, bf16[48,1152]{1,0:T(8,128)(2,1)S(1)}, u32[]{:S(2)}, u32[]{:S(2)}) collective-permute-start(bf16[48,1152]{1,0:T(8,128)(2,1)S(1)} %get-tuple-element.45), channel_id=1, source_target_pairs={{0,8},{4,12},{8,0},{12,4},{16,24},{20,28},{24,16},{28,20},{1,9},{5... | collective-permute-start | bytes 331784 | tf_op jit(solution)/shard_map/ppermute | solution.py:400
  4.7 13.7 %collective-permute-start.1 = (bf16[48,1152]{1,0:T(8,128)(2,1)S(1)}, bf16[48,1152]{1,0:T(8,128)(2,1)S(1)}, u32[]{:S(2)}, u32[]{:S(2)}) collective-permute-start(bf16[48,1152]{1,0:T(8,128)(2,1)S(1)} %get-tuple-element.45), channel_id=1, source_target_pairs={{0,16},{4,20},{8,24},{12,28},{16,0},{20,4},{24,8},{28,12},{1,17},{... | collective-permute-start | bytes 331784 | tf_op jit(solution)/shard_map/ppermute | solution.py:400
  7.3 11.1 %collective-permute-start.2 = (bf16[48,1152]{1,0:T(8,128)(2,1)S(1)}, bf16[48,1152]{1,0:T(8,128)(2,1)S(1)}, u32[]{:S(2)}, u32[]{:S(2)}) collective-permute-start(bf16[48,1152]{1,0:T(8,128)(2,1)S(1)} %get-tuple-element.45), channel_id=1, source_target_pairs={{0,24},{4,28},{8,16},{12,20},{16,8},{20,12},{24,0},{28,4},{1,25},{... | collective-permute-start | bytes 331784 | tf_op jit(solution)/shard_map/ppermute | solution.py:400
  7.3 11.1 %collective-permute-start.3 = (bf16[48,1152]{1,0:T(8,128)(2,1)S(1)}, bf16[48,1152]{1,0:T(8,128)(2,1)S(1)}, u32[]{:S(2)}, u32[]{:S(2)}) collective-permute-start(bf16[48,1152]{1,0:T(8,128)(2,1)S(1)} %get-tuple-element.45), channel_id=1, source_target_pairs={{0,4},{4,0},{8,12},{12,8},{16,20},{20,16},{24,28},{28,24},{1,5},{5... | collective-permute-start | bytes 331784 | tf_op jit(solution)/shard_map/ppermute | solution.py:400
  9.0 9.4 %collective-permute-start.4 = (bf16[48,1152]{1,0:T(8,128)(2,1)S(1)}, bf16[48,1152]{1,0:T(8,128)(2,1)S(1)}, u32[]{:S(2)}, u32[]{:S(2)}) collective-permute-start(bf16[48,1152]{1,0:T(8,128)(2,1)S(1)} %get-tuple-element.45), channel_id=1, source_target_pairs={{0,12},{4,8},{8,4},{12,0},{16,28},{20,24},{24,20},{28,16},{1,13},{... | collective-permute-start | bytes 331784 | tf_op jit(solution)/shard_map/ppermute | solution.py:400
  18.5 2.0 %collective-permute-start.5 = (bf16[240,1152]{1,0:T(8,128)(2,1)S(1)}, bf16[240,1152]{1,0:T(8,128)(2,1)S(1)}, u32[]{:S(2)}, u32[]{:S(2)}) collective-permute-start(bf16[240,1152]{1,0:T(8,128)(2,1)S(1)} %constant_dynamic-update-slice_fusion), channel_id=1, source_target_pairs={{0,1},{1,0},{2,3},{3,2},{4,5},{5,4},{6,7},{7,6},{8,9},{9,8},{10,11... | collective-permute-start | bytes 1658888 | tf_op jit(solution)/shard_map/ppermute | solution.py:397
  18.6 7.9 %collective-permute-start.6 = (bf16[96,1152]{1,0:T(8,128)(2,1)S(1)}, bf16[96,1152]{1,0:T(8,128)(2,1)S(1)}, u32[]{:S(2)}, u32[]{:S(2)}) collective-permute-start(bf16[96,1152]{1,0:T(8,128)(2,1)S(1)} %pad_maximum_fusion), channel_id=1, source_target_pairs={{0,4},{4,0},{8,12},{12,8},{16,20},{20,16},{24,28},{28,24},{1,5},{5... | collective-permute-start | bytes 663560 | tf_op jit(solution)/shard_map/ppermute | solution.py:400
  26.5 1.5 %collective-permute-start.7 = (bf16[96,1152]{1,0:T(8,128)(2,1)S(1)}, bf16[96,1152]{1,0:T(8,128)(2,1)S(1)}, u32[]{:S(2)}, u32[]{:S(2)}) collective-permute-start(bf16[96,1152]{1,0:T(8,128)(2,1)S(1)} %collective-permute-done.6), channel_id=1, source_target_pairs={{0,1},{1,0},{2,3},{3,2},{4,5},{5,4},{6,7},{7,6},{8,9},{9,8},{10,11... | collective-permute-start | bytes 663560 | tf_op jit(solution)/shard_map/ppermute | solution.py:397
  32.7 6.2 %collective-permute-start.10 = (f32[2,768]{1,0:T(2,128)S(1)}, f32[2,768]{1,0:T(2,128)S(1)}, u32[]{:S(2)}, u32[]{:S(2)}) collective-permute-start(f32[2,768]{1,0:T(2,128)S(1)} %maximum_maximum_fusion), channel_id=1, source_target_pairs={{0,3},{1,2},{2,1},{3,0},{4,7},{5,6},{6,5},{7,4},{8,11},{9,10},{10,... | collective-permute-start | bytes 18440 | tf_op jit(solution)/shard_map/ppermute | solution.py:437
  34.2 4.8 %collective-permute-start.8 = (f32[2,768]{1,0:T(2,128)S(1)}, f32[2,768]{1,0:T(2,128)S(1)}, u32[]{:S(2)}, u32[]{:S(2)}) collective-permute-start(f32[2,768]{1,0:T(2,128)S(1)} %maximum_maximum_fusion), channel_id=1, source_target_pairs={{0,1},{1,0},{2,3},{3,2},{4,5},{5,4},{6,7},{7,6},{8,9},{9,8},{10,11... | collective-permute-start | bytes 18440 | tf_op jit(solution)/shard_map/ppermute | solution.py:437
  34.5 4.4 %collective-permute-start.9 = (f32[2,768]{1,0:T(2,128)S(1)}, f32[2,768]{1,0:T(2,128)S(1)}, u32[]{:S(2)}, u32[]{:S(2)}) collective-permute-start(f32[2,768]{1,0:T(2,128)S(1)} %maximum_maximum_fusion), channel_id=1, source_target_pairs={{0,2},{1,3},{2,0},{3,1},{4,6},{5,7},{6,4},{7,5},{8,10},{9,11},{10,... | collective-permute-start | bytes 18440 | tf_op jit(solution)/shard_map/ppermute | solution.py:437
where the time goes:
time: 44.2 us; the launch traced here: 44 us
  Pallas kernels  29.3 us (66%)
  starting transfers between devices  12.2 us (28%)
  waiting for transfers between devices  1.85 us (4%)
    pallas_call x3, Pallas kernels, powers_of(): pl.pallas_call(functools.partial(powers_kernel, tiles, min_live, depth, f...  15.9 us
    ppermute x6, starting transfers between devices, exchange(): return lax.ppermute(x, 'img', [(i, i ^ step) for i in range(n_img)])  9.62 us
    pallas_call x1, Pallas kernels, applied(): pl.pallas_call(functools.partial(apply_kernel, tiles, len(tops), len(far)...  4.84 us
    pallas_call x1, Pallas kernels, graph_of(): pl.pallas_call(functools.partial(graph_kernel, order, k), in_specs=[SCALA...  3.85 us
    pallas_call x1, Pallas kernels, prepared(): pl.pallas_call(functools.partial(prepare_kernel, order, total_rows), in_s...  3.22 us
    ppermute x3, starting transfers between devices, shards(): lax.ppermute(stats, 'cls', [(i, i ^ d) for i in range(n_cls)])  2.39 us
    ppermute x2, waiting for transfers between devices, swap(): return lax.ppermute(x, 'cls', [(i, i ^ 1) for i in range(n_cls)])  1.7 us
    pallas_call x1, Pallas kernels, tables_of(): pl.pallas_call(table_kernel, in_specs=[SCALARS] + [HBM] * 4, out_specs=[W...  1.52 us
  transfers between devices with their start and end apart: 11, of which 3 were waited for; matrix products, arithmetic and copies ran while one was open for 0% of the time, Pallas kernels for 42%

commit v1 on v0

v1 whole, which is shorter than its diff:
```python
import functools
import jax
import jax.numpy as jnp
from jax import lax
from jax.experimental import pallas as pl
from jax.experimental.pallas import tpu as pltpu
from jax.sharding import PartitionSpec as P

LIVE = 21841
SMOOTHING = 1.0
TILE = 512
LANES = 128
HALF = LANES // 2
DEEP = 3
NT = (((1,), (1,)), ((), ()))
GROUP = 128
f32, bf16 = jnp.float32, jnp.bfloat16
VMEM = pltpu.VMEM
WHOLE = pl.BlockSpec(memory_space=VMEM)
SCALARS = pl.BlockSpec(memory_space=pltpu.SMEM)
ANYWHERE = pl.BlockSpec(memory_space=pl.ANY)
MIB = 2**20
FREE = pl.CostEstimate(flops=1000, bytes_accessed=1000, transcendentals=0)


def column_tiles(width):
    return [(a, min(a + TILE, width)) for a in range(0, width, TILE)]


def round_up(n, m):
    return -(-n // m) * m


def resident(x):
    return pltpu.with_memory_space_constraint(x, VMEM)


def exchange_plan(peers):
    direct = list(range(2, peers, 2))

    def cut(blocks):
        return [blocks[i : i + 4] for i in range(0, len(blocks), 4)]

    return [2] + direct[1:] + [3, 1], direct[1:], cut(direct + [1]), cut([3] + [b ^ 1 for b in direct[1:]])


def outside(x):
    return pltpu.with_memory_space_constraint(x, pltpu.HBM)


HBM = pl.BlockSpec(memory_space=pltpu.HBM)


def table_kernel(here_ref, requests_hbm, e_hbm, neighbours_hbm, weights_hbm, own_ref, mine_ref, table_ref, near_ref, weight_ref, requests_ref, sems):
    core, me = here_ref[1], here_ref[2]
    rows, depth = e_hbm.shape
    half = rows // 2
    peers, cap = requests_hbm.shape
    k = near_ref.shape[0]
    slots = round_up(k, 8)
    start = pl.multiple_of(core * half, 16)
    moves = (
        (requests_hbm, requests_ref),
        (neighbours_hbm, near_ref),
        (weights_hbm, weight_ref),
        (e_hbm.at[pl.ds(start, half), :], mine_ref.at[:, :depth]),
        (e_hbm, own_ref.at[:, :depth]),
    )
    copies = [pltpu.make_async_copy(src, dst, sems.at[i]) for i, (src, dst) in enumerate(moves)]
    for copy in copies:
        copy.start()
    table_ref[...] = jnp.zeros_like(table_ref)
    for copy in copies[:3]:
        copy.wait()
    near = near_ref[...]
    slot = near - rows
    block = jnp.zeros_like(near) + me
    within = near
    for p in range(peers):
        block = jnp.where(slot >= p * cap, p, block)
        for j in range(cap):
            within = jnp.where(slot == p * cap + j, requests_ref[p, j], within)
    weight = weight_ref[...]
    w0 = weight.astype(bf16).astype(f32)
    w1 = (weight - w0).astype(bf16).astype(f32)
    w2 = weight - w0 - w1
    for i, x in enumerate((block.astype(f32), within.astype(f32), w0, w1, w2)):
        table_ref[i * slots : i * slots + k, :] = x
    own_ref[:, depth:] = table_ref[...].T.astype(bf16)
    mine_ref[:, depth:] = own_ref[pl.ds(start, half), depth:]
    for copy in copies[3:]:
        copy.wait()


def tables_of(here, requests, embeddings, neighbours, weights):
    rows, depth = embeddings.shape
    k = neighbours.shape[1]
    return pl.pallas_call(
        table_kernel,
        in_specs=[SCALARS] + [HBM] * 4,
        out_specs=[WHOLE] * 2,
        out_shape=[VMEM((rows, depth + LANES), bf16), VMEM((rows // 2, depth + LANES), bf16)],
        scratch_shapes=[
            VMEM((LANES, rows), f32),
            VMEM((k, rows), jnp.int32),
            VMEM((k, rows), f32),
            pltpu.SMEM(requests.shape, jnp.int32),
            pltpu.SemaphoreType.DMA((5,)),
        ],
        compiler_params=pltpu.CompilerParams(vmem_limit_bytes=MIB),
        cost_estimate=pl.CostEstimate(flops=3 * 10**10, bytes_accessed=10**8, transcendentals=0),
        name="tables",
    )(here, outside(requests), outside(embeddings), outside(neighbours.T), outside(weights.T))


def split(x):
    hi = x.astype(bf16)
    return hi, (x - hi.astype(f32)).astype(bf16)


def dot(a, b):
    return jnp.dot(a, b, preferred_element_type=f32)


def add_powers(tiles, min_live, here_ref, e_ref, ct_ref, p_ref, rows, stat_ref, before=None):
    n = e_ref.shape[0]
    lane = lax.broadcasted_iota(jnp.int32, (n, LANES), 1)
    stat = jnp.where(lane < HALF, -1e30, 0.0)
    for t, (a, b) in enumerate(tiles):
        if before:
            before(t)
        logits = lax.dot_general(e_ref[...], ct_ref[a:b, :], NT, preferred_element_type=f32)
        if b > min_live:
            live = lax.broadcasted_iota(jnp.int32, logits.shape, 1) + a < here_ref[0]
            logits = jnp.where(live, logits, -1e30)
        top = jnp.max(logits, axis=1, keepdims=True)
        powers = jnp.exp(logits - top)
        if b > min_live:
            powers = jnp.where(live, powers, 0.0)
        p_ref[rows, a:b] = powers
        stat = jnp.where(lane == t, top, stat)
        stat = jnp.where(lane == t + HALF, jnp.sum(powers, axis=1, keepdims=True), stat)
    stat_ref[rows, :] = stat
    return stat


def row_stats(stat, slots):
    turned = stat.T
    tops, sums = turned[:slots], turned[HALF : HALF + slots]
    top = jnp.max(tops, axis=0, keepdims=True)
    return tops, jnp.concatenate([top, jnp.sum(sums * jnp.exp(tops - top), axis=0, keepdims=True)], axis=0)


def powers_kernel(tiles, min_live, depth, first_row, n_parts, final, here_ref, *refs):
    parts, ct_ref = refs[:n_parts], refs[n_parts]
    p_ref, tab_ref, stat_ref, *ends, e_ref = refs[n_parts + 4 :]
    if final:
        tile_ref, both_ref = ends
        slots = tile_ref.shape[0]
        tops, both = row_stats(stat_ref[:first_row, :], slots)
    core = here_ref[1]
    row = 0
    for i, part in enumerate(parts):
        n = part.shape[0]
        at = pl.multiple_of(row + n * (-core if i % 2 else core), 16)
        e_ref[pl.ds(at, n), :] = part[:, :depth]
        tab_ref[pl.ds(first_row + at, n), :] = part[:, depth:].astype(f32)
        row += n
    stat = add_powers(tiles, min_live, here_ref, e_ref, ct_ref, p_ref, slice(first_row, first_row + row), stat_ref)
    if final:
        own_tops, own_both = row_stats(stat, slots)
        tile_ref[...] = jnp.concatenate([tops, own_tops], axis=1)
        both_ref[...] = jnp.concatenate([both, own_both], axis=1)


def powers_shapes(total_rows, width):
    return [VMEM((total_rows, width), f32), VMEM((total_rows, LANES), f32), VMEM((total_rows, LANES), f32)]


def powers_of(parts, ct, here, buffers, first_row, min_live):
    width, depth = ct.shape
    rows = sum(p.shape[0] for p in parts)
    total_rows = buffers[0].shape[0]
    tiles = column_tiles(width)
    final = first_row + rows == total_rows
    n = len(parts)
    shapes = powers_shapes(total_rows, width)
    if final:
        shapes += [VMEM((round_up(len(tiles), 8), total_rows), f32), VMEM((2, total_rows), f32)]
    return pl.pallas_call(
        functools.partial(powers_kernel, tiles, min_live, depth, first_row, n, final),
        in_specs=[SCALARS] + [WHOLE] * (n + 4),
        out_specs=[WHOLE] * len(shapes),
        out_shape=shapes,
        scratch_shapes=[VMEM((rows, depth), bf16)],
        input_output_aliases={2 + n + i: i for i in range(3)},
        compiler_params=pltpu.CompilerParams(vmem_limit_bytes=8 * MIB),
        cost_estimate=FREE,
        name="powers",
    )(here, *[resident(x) for x in parts], ct, *[resident(x) for x in buffers])


def place_of(order, rows_here, me, block, within):
    relative = block ^ me
    place = jnp.zeros_like(block)
    for i, b in enumerate(order):
        place = jnp.where(relative == b, i * rows_here, place)
    return place + within


def own_kernel(tiles, min_live, order, here_ref, own_ref, ct_ref, requests_hbm, near_hbm, weight_hbm, *refs):
    p_ref, tab_ref, stat_ref, whi_ref, wlo_ref, scale_ref, asked_ref, pick_ref = refs[:8]
    e_ref, row_ref, near_ref, weight_ref, requests_ref, sems = refs[8:]
    me = here_ref[2]
    peers, cap = requests_hbm.shape
    k, rows_here = near_hbm.shape
    total_rows = tab_ref.shape[0]
    moves = (
        (requests_hbm, requests_ref),
        (near_hbm, near_ref),
        (weight_hbm, weight_ref),
    )
    copies = [pltpu.make_async_copy(src, dst, sems.at[i]) for i, (src, dst) in enumerate(moves)]
    for copy in copies:
        copy.start()
    depth = e_ref.shape[1]
    e_ref[...] = own_ref[:, :depth]
    tab_ref[:rows_here, :] = own_ref[:, depth:].astype(f32)
    row_ref[...] = jnp.full_like(row_ref, -1)
    for copy in copies:
        copy.wait()

    def edges():
        lane = lax.broadcasted_iota(jnp.int32, (1, LANES), 1)
        for p in range(peers):
            start = place_of(order, rows_here, me, jnp.full((1, 1), p, jnp.int32), 0)
            row = jnp.full((1, LANES), -1, jnp.int32)
            for j in range(cap):
                row = jnp.where(lane == j, requests_ref[p, j], row)
            row_ref[p : p + 1, :] = jnp.where(row >= 0, row + start, -1)
        asked = row_ref[...].T
        column = lax.broadcasted_iota(jnp.int32, (cap, total_rows), 1)
        for p in range(peers):
            one = asked[:cap, p : p + 1]
            asked_ref[p * cap : (p + 1) * cap, :] = jnp.broadcast_to(one, (cap, LANES))
            pick_ref[p * cap : (p + 1) * cap, :] = jnp.where(column == one, 1.0, 0.0).astype(bf16)
        near, weight = near_ref[...].T, weight_ref[...].T
        column = lax.broadcasted_iota(jnp.int32, whi_ref.shape, 1)
        acc = jnp.zeros(whi_ref.shape, f32)
        for i in range(k):
            acc = acc + jnp.where(column == near[:, i : i + 1], SMOOTHING * weight[:, i : i + 1], 0.0)
        scale = 1.0 / (1.0 + SMOOTHING * jnp.sum(weight, axis=1, keepdims=True))
        whi_ref[...], wlo_ref[...] = split(acc * scale)
        scale_ref[...] = jnp.broadcast_to(scale, scale_ref.shape)

    edges()
    add_powers(tiles, min_live, here_ref, e_ref, ct_ref, p_ref, slice(0, rows_here), stat_ref)


def own_powers(here, own, requests, neighbours, weights, classes, order, total_rows, min_live):
    rows_here = own.shape[0]
    width, depth = classes.shape
    k = neighbours.shape[1]
    extended = rows_here + requests.size
    tiles = column_tiles(width)
    shapes = powers_shapes(total_rows, width) + [
        VMEM((rows_here, extended), bf16),
        VMEM((rows_here, extended), bf16),
        VMEM((rows_here, LANES), f32),
        VMEM((requests.size, LANES), jnp.int32),
        VMEM((requests.size, total_rows), bf16),
    ]
    return pl.pallas_call(
        functools.partial(own_kernel, tiles, min_live, order),
        in_specs=[SCALARS, WHOLE, WHOLE] + [HBM] * 3,
        out_specs=[WHOLE] * len(shapes),
        out_shape=shapes,
        scratch_shapes=[
            VMEM((rows_here, depth), bf16),
            VMEM((LANES, LANES), jnp.int32),
            VMEM((k, rows_here), jnp.int32),
            VMEM((k, rows_here), f32),
            pltpu.SMEM(requests.shape, jnp.int32),
            pltpu.SemaphoreType.DMA((3,)),
        ],
        compiler_params=pltpu.CompilerParams(vmem_limit_bytes=8 * MIB),
        cost_estimate=FREE,
        name="own",
    )(here, resident(own), classes, *[outside(x) for x in (requests, neighbours.T, weights.T)])


def spans(rows_here, extended):
    return [(0, rows_here)] + [(a, min(GROUP, extended - a)) for a in range(rows_here, extended, GROUP)]


def graph_kernel(order, k, here_ref, whi_ref, wlo_ref, scale_ref, asked_ref, pick_ref, tab_ref, m_ref, rows_ref, thi_ref, tlo_ref):
    me = here_ref[2]
    total_rows = tab_ref.shape[0]
    rows_here, extended = whi_ref.shape
    slots = round_up(k, 8)
    rows_ref[rows_here:, :] = dot(pick_ref[...], tab_ref[...].astype(bf16))
    for start, size in spans(rows_here, extended):
        column = lax.broadcasted_iota(jnp.int32, (size, total_rows), 1)
        tab = tab_ref[:rows_here, :] if start < rows_here else rows_ref[start : start + size, :]
        within = pltpu.roll(tab, LANES - slots, 1).astype(jnp.int32)
        weight = pltpu.roll(tab, LANES - 2 * slots, 1) + pltpu.roll(tab, LANES - 3 * slots, 1) + pltpu.roll(tab, LANES - 4 * slots, 1)
        place = place_of(order, rows_here, me, tab.astype(jnp.int32), within)
        itself = lax.broadcasted_iota(jnp.int32, (size, LANES), 0) if start < rows_here else asked_ref[start - rows_here : start - rows_here + size, :]
        acc = jnp.where(column == itself[:, :1], 1.0, 0.0)
        degree = jnp.zeros((size, 1), f32)
        for i in range(k):
            w = weight[:, i : i + 1]
            acc = acc + jnp.where(column == place[:, i : i + 1], SMOOTHING * w, 0.0)
            degree = degree + w
        thi_ref[start : start + size, :], tlo_ref[start : start + size, :] = split(acc * (1.0 / (1.0 + SMOOTHING * degree)))
    column = lax.broadcasted_iota(jnp.int32, (rows_here, total_rows), 1)
    sub = lax.broadcasted_iota(jnp.int32, (rows_here, total_rows), 0)
    own = jnp.where(column == sub, scale_ref[:, :1], 0.0)
    thi = thi_ref[...]
    m_ref[...] = own + dot(whi_ref[...], thi) + dot(wlo_ref[...], thi) + dot(whi_ref[...], tlo_ref[...])


def graph_of(here, edges, tab, order, k):
    total_rows = tab.shape[0]
    rows_here, extended = edges[0].shape
    return pl.pallas_call(
        functools.partial(graph_kernel, order, k),
        in_specs=[SCALARS] + [WHOLE] * 6,
        out_specs=WHOLE,
        out_shape=VMEM((rows_here, total_rows), f32),
        scratch_shapes=[VMEM((extended, LANES), f32), VMEM((extended, total_rows), bf16), VMEM((extended, total_rows), bf16)],
        compiler_params=pltpu.CompilerParams(vmem_limit_bytes=(6 if total_rows <= 768 else 20) * MIB),
        cost_estimate=FREE,
        name="graph",
    )(here, *[resident(x) for x in edges], resident(tab))


def apply_kernel(tiles, m_ref, p_ref, tile_ref, *refs):
    *stat_refs, out_ref, _, staged, sems = refs
    rows_here = m_ref.shape[0]
    tops, sums = [r[0:1, :] for r in stat_refs], [r[1:2, :] for r in stat_refs]
    top = functools.reduce(jnp.maximum, tops)
    total = sum(s * jnp.exp(t - top) for s, t in zip(sums, tops))
    factors = jnp.exp(tile_ref[...] - top) / total
    copies = []
    for t, (a, b) in enumerate(tiles):
        whi, wlo = split(m_ref[...] * factors[t : t + 1, :])
        hi, lo = split(p_ref[:, a:b])
        x = dot(jnp.concatenate([whi, wlo], axis=0), hi)
        staged[:, a:b] = x[:rows_here] + x[rows_here:] + dot(whi, lo)
        copy = pltpu.make_async_copy(staged.at[:, a:b], out_ref.at[:, a:b], sems.at[t])
        copy.start()
        copies.append(copy)
    for copy in copies:
        copy.wait()


def applied(m, powers, tile_tops, stats, far):
    rows_here, width = m.shape[0], powers.shape[1]
    total_rows = m.shape[1]
    tiles = column_tiles(width)
    operands = [m, powers, tile_tops, stats, *far]
    return pl.pallas_call(
        functools.partial(apply_kernel, tiles),
        in_specs=[WHOLE] * len(operands),
        out_specs=[ANYWHERE, WHOLE],
        out_shape=[jax.ShapeDtypeStruct((rows_here, width), f32), VMEM(powers.shape, f32)],
        input_output_aliases={1: 1},
        scratch_shapes=[VMEM((rows_here, width), f32), pltpu.SemaphoreType.DMA((len(tiles),))],
        compiler_params=pltpu.CompilerParams(vmem_limit_bytes=(8 if total_rows <= 768 else 16) * MIB),
        cost_estimate=FREE,
        name="smooth",
    )(*[resident(x) for x in operands])[0]


def shards(n_img, n_cls, embeddings, class_text_embedding, neighbours, weights, requests):
    rows_here = embeddings.shape[0]
    width = class_text_embedding.shape[1]
    half = rows_here // 2
    me, col = lax.axis_index("img"), lax.axis_index("cls")
    total_rows = n_img * rows_here
    here = jnp.stack([jnp.minimum(LIVE - col * width, width), col & 1, me]).astype(jnp.int32)
    min_live = min(width, LIVE - (n_cls - 1) * width)

    classes = class_text_embedding.T
    own, mine = tables_of(here, requests[0], embeddings, neighbours, weights)
    first, relayed, beside, last = exchange_plan(n_img)
    order = [0] + [b for piece in beside + last for b in piece]

    def swap(x):
        return lax.ppermute(x, "cls", [(i, i ^ 1) for i in range(n_cls)])

    def exchange(x, step):
        return lax.ppermute(x, "img", [(i, i ^ step) for i in range(n_img)])

    def halves(x, blocks):
        other = swap(x)
        cuts = [slice(i * half, (i + 1) * half) for i in range(len(blocks))]
        return {b: [x[c], other[c]] for b, c in zip(blocks, cuts)}

    held = [exchange(mine, b) for b in first]
    results = own_powers(here, own, requests[0], neighbours, weights, classes, order, total_rows, min_live)
    buffers, first_row, edges = list(results[:3]), rows_here, results[3:]

    def work(blocks):
        nonlocal buffers, first_row
        parts = [x for b in blocks for x in pairs[b]]
        buffers = list(powers_of(parts, classes, here, buffers, first_row, min_live))
        first_row += len(blocks) * rows_here

    *held, buffers[2] = lax.optimization_barrier((*held, buffers[2]))
    got = exchange(jnp.concatenate([x for b, x in zip(first, held) if b in relayed], axis=0), 1)
    pairs = halves(jnp.concatenate(held, axis=0), first)
    for piece in beside:
        work(piece)
    got, buffers[2] = lax.optimization_barrier((got, buffers[2]))
    pairs |= halves(got, [b ^ 1 for b in relayed])
    for piece in last:
        work(piece)
    powers, tab, _, tile_tops, stats = buffers
    far = [lax.ppermute(stats, "cls", [(i, i ^ d) for i in range(n_cls)]) for d in range(1, n_cls)]
    m = graph_of(here, edges, tab, order, neighbours.shape[1])
    return applied(m, powers, tile_tops, stats, far)


def solution(mesh):
    in_specs = (
        P("img", None),
        P(None, "cls"),
        P("img", None),
        P("img", None),
        P("img", None, None),
    )
    sizes = mesh.shape
    run = functools.partial(shards, sizes["img"], sizes["cls"])
    return jax.shard_map(run, mesh=mesh, in_specs=in_specs, out_specs=P("img", "cls"), check_vma=False)
```

time: 44.2 us -> 41.2 us (0.932)
  Pallas kernels: 29.3 us -> 25.3 us
  waiting for transfers between devices: 1.85 us -> 3.29 us
    pallas_call x3 -> x2, Pallas kernels: 15.9 us -> 10.2 us  [powers_of(): pl.pallas_call(functools.partial(powers_kernel, tiles, min_live, depth, f...]
    pallas_call x2, Pallas kernels: 8.05 us -> 10 us  [the longest x1 5.11 us: own_powers(): pl.pallas_call(functools.partial(own_kernel, tiles, min_live, order), in_...]
    ppermute x6, waiting for transfers between devices: 0.14 us -> 1.55 us  [exchange(): return lax.ppermute(x, 'img', [(i, i ^ step) for i in range(n_img)])]
    pallas_call x1, Pallas kernels: 3.85 us -> 3.21 us  [graph_of(): pl.pallas_call(functools.partial(graph_kernel, order, k), in_specs=[SCALA...]
  transfers between devices with their start and end apart: 11 -> 11, of which waited for: 3 -> 4; matrix products, arithmetic and copies ran while one was open for 0% -> 0% of each run, Pallas kernels for 42% -> 34%
where the time goes in v1:
time: 41.2 us; the launch traced here: 41 us
  Pallas kernels  25.3 us (61%)
  starting transfers between devices  11.9 us (29%)
  waiting for transfers between devices  3.29 us (8%)
    pallas_call x2, Pallas kernels, powers_of(): pl.pallas_call(functools.partial(powers_kernel, tiles, min_live, depth, f...  10.2 us
    ppermute x6, starting transfers between devices, exchange(): return lax.ppermute(x, 'img', [(i, i ^ step) for i in range(n_img)])  9.67 us
    pallas_call x1, Pallas kernels, own_powers(): pl.pallas_call(functools.partial(own_kernel, tiles, min_live, order), in_...  5.11 us
    pallas_call x1, Pallas kernels, applied(): pl.pallas_call(functools.partial(apply_kernel, tiles), in_specs=[WHOLE] *...  4.89 us
    pallas_call x1, Pallas kernels, graph_of(): pl.pallas_call(functools.partial(graph_kernel, order, k), in_specs=[SCALA...  3.21 us
    ppermute x3, starting transfers between devices, shards(): lax.ppermute(stats, 'cls', [(i, i ^ d) for i in range(n_cls)])  2.18 us
    pallas_call x1, Pallas kernels, tables_of(): pl.pallas_call(table_kernel, in_specs=[SCALARS] + [HBM] * 4, out_specs=[W...  1.82 us
    ppermute x2, waiting for transfers between devices, swap(): return lax.ppermute(x, 'cls', [(i, i ^ 1) for i in range(n_cls)])  1.73 us
  transfers between devices with their start and end apart: 11, of which 4 were waited for; matrix products, arithmetic and copies ran while one was open for 0% of the time, Pallas kernels for 34%

profile of v1, /device:TPU:0, one launch (start us, length us, event | category | flops | bytes accessed | tf_op | source)
XLA Modules:
  0.0 41.0 jit_solution(6509279736269283315)
XLA Ops:
  0.0 0.1 pad_add_fusion.here_ref
  0.1 0.0 copy-start
  0.1 1.8 %tables.1 = (bf16[96,1152]{1,0:T(8,128)(2,1)S(1)}, bf16[48,1152]{1,0:T(8,128)(2,1)S(1)}) custom-call(s32[3]{0:T(128)S(1)} %pad_add_fusion.here_ref, s32[8,16]{1,0:T(8,128)} %bitcast.14, bf16[96,1024]{1,0:T(8,128)(2,1)} %e_hbm.1, s32[10,96]{1,0:T(8,128)} %bitcast.10, f32[10,96]{1,0:T(8,128)} %bitcast.12), custom_call_target="tpu_custom_call" | custom-call | flops 30000001024 | bytes 100000000 | tf_op jit(solution)/shard_map/tables/pallas_call | solution.py:98
  1.9 3.1 %collective-permute-start = (bf16[48,1152]{1,0:T(8,128)(2,1)S(1)}, bf16[48,1152]{1,0:T(8,128)(2,1)S(1)}, u32[]{:S(2)}, u32[]{:S(2)}) collective-permute-start(bf16[48,1152]{1,0:T(8,128)(2,1)S(1)} %get-tuple-element.37), channel_id=1, source_target_pairs={{0,8},{4,12},{8,0},{12,4},{16,24},{20,28},{24,16},{28,20},{1,9},{5... | collective-permute-start | bytes 331784 | tf_op jit(solution)/shard_map/ppermute | solution.py:394
  5.0 2.6 %collective-permute-start.1 = (bf16[48,1152]{1,0:T(8,128)(2,1)S(1)}, bf16[48,1152]{1,0:T(8,128)(2,1)S(1)}, u32[]{:S(2)}, u32[]{:S(2)}) collective-permute-start(bf16[48,1152]{1,0:T(8,128)(2,1)S(1)} %get-tuple-element.37), channel_id=1, source_target_pairs={{0,16},{4,20},{8,24},{12,28},{16,0},{20,4},{24,8},{28,12},{1,17},{... | collective-permute-start | bytes 331784 | tf_op jit(solution)/shard_map/ppermute | solution.py:394
  7.6 0.0 collective-permute-start.2
  7.6 1.9 %collective-permute-start.3 = (bf16[48,1152]{1,0:T(8,128)(2,1)S(1)}, bf16[48,1152]{1,0:T(8,128)(2,1)S(1)}, u32[]{:S(2)}, u32[]{:S(2)}) collective-permute-start(bf16[48,1152]{1,0:T(8,128)(2,1)S(1)} %get-tuple-element.37), channel_id=1, source_target_pairs={{0,12},{4,8},{8,4},{12,0},{16,28},{20,24},{24,20},{28,16},{1,13},{... | collective-permute-start | bytes 331784 | tf_op jit(solution)/shard_map/ppermute | solution.py:394
  9.4 0.5 %collective-permute-start.4 = (bf16[48,1152]{1,0:T(8,128)(2,1)S(1)}, bf16[48,1152]{1,0:T(8,128)(2,1)S(1)}, u32[]{:S(2)}, u32[]{:S(2)}) collective-permute-start(bf16[48,1152]{1,0:T(8,128)(2,1)S(1)} %get-tuple-element.37), channel_id=1, source_target_pairs={{0,4},{4,0},{8,12},{12,8},{16,20},{20,16},{24,28},{28,24},{1,5},{5... | collective-permute-start | bytes 331784 | tf_op jit(solution)/shard_map/ppermute | solution.py:394
  9.9 0.0 copy-done
  9.9 5.1 %own.1 = (f32[768,5472]{1,0:T(8,128)S(1)}, f32[768,128]{1,0:T(8,128)S(1)}, f32[768,128]{1,0:T(8,128)S(1)}, bf16[96,224]{1,0:T(8,128)(2,1)S(1)}, bf16[96,224]{1,0...) custom-call(s32[3]{0:T(128)S(1)} %pad_add_fusion.here_ref, ...), custom_call_target="tpu_custom_call" | custom-call | flops 1000 | bytes 1000 | tf_op jit(solution)/shard_map/own/pallas_call | solution.py:273
  15.1 0.0 collective-permute-done.refs_0_
  15.1 1.3 %collective-permute-done.1.refs_2_ = bf16[48,1152]{1,0:T(8,128)(2,1)S(1)} collective-permute-done((bf16[48,1152]{1,0:T(8,128)(2,1)S(1)}, bf16[48,1152]{1,0:T(8,128)(2,1)S(1)}, u32[]{:S(2)}, u32[]{:S(2)}) %collective-permute-start.1) | collective-permute-done | bytes 110624 | tf_op jit(solution)/shard_map/ppermute | solution.py:394
  16.3 0.0 collective-permute-done.2.refs_4_
  16.3 0.0 collective-permute-done.3.refs_0_
  16.3 0.0 collective-permute-done.4.refs_6_
  16.5 0.1 collective-permute-start.5
  16.6 1.6 %collective-permute-start.6 = (bf16[96,1152]{1,0:T(8,128)(2,1)S(1)}, bf16[96,1152]{1,0:T(8,128)(2,1)S(1)}, u32[]{:S(2)}, u32[]{:S(2)}) collective-permute-start(bf16[96,1152]{1,0:T(8,128)(2,1)S(1)} %pad_maximum_fusion), channel_id=1, source_target_pairs={{0,4},{4,0},{8,12},{12,8},{16,20},{20,16},{24,28},{28,24},{1,5},{5... | collective-permute-start | bytes 663560 | tf_op jit(solution)/shard_map/ppermute | solution.py:394
  18.2 0.3 collective-permute-done.5
  18.5 5.6 %powers.2 = (f32[768,5472]{1,0:T(8,128)S(1)}, f32[768,128]{1,0:T(8,128)S(1)}, f32[768,128]{1,0:T(8,128)S(1)}) custom-call(s32[3]{0:T(128)S(1)} %pad_add_fusion.here_ref, bf16[48,1152]{1,0:T(8,128)(2,1)S(1)} %collective-permute-done.refs_0_, ...), custom_call_target="tpu_custom_call", output_to_operand_aliasing={{0}: (10, {}), {1}: (11, {}), {2}: (12, {})} | custom-call | flops 1000 | bytes 1000 | tf_op jit(solution)/shard_map/powers/pallas_call | solution.py:190
  24.2 0.3 collective-permute-done.6
  24.5 0.0 collective-permute-start.7
  24.5 1.5 %collective-permute-done.7 = bf16[96,1152]{1,0:T(8,128)(2,1)S(1)} collective-permute-done((bf16[96,1152]{1,0:T(8,128)(2,1)S(1)}, bf16[96,1152]{1,0:T(8,128)(2,1)S(1)}, u32[]{:S(2)}, u32[]{:S(2)}) %collective-permute-start.7) | collective-permute-done | bytes 221216 | tf_op jit(solution)/shard_map/ppermute | solution.py:391
  26.0 4.6 %powers.3 = (f32[768,5472]{1,0:T(8,128)S(1)}, f32[768,128]{1,0:T(8,128)S(1)}, f32[768,128]{1,0:T(8,128)S(1)}, f32[16,768]{1,0:T(8,128)S(1)}, f32[2,768]{1,0:T(2,128)S(1)}) custom-call(s32[3]{0:T(128)S(1)} %pad_add_fusion.here_ref, bf16[48,1152]{1,0:T(8,128)(2,1)S(1)} %collective-permute-done.3.refs_0_, ...), custom_call_target="tpu_custom_call", output_to_operand_aliasing={{0}: (8, {}), {1}: (9, {}), {2}: (10, {})} | custom-call | flops 1000 | bytes 1000 | tf_op jit(solution)/shard_map/powers/pallas_call | solution.py:190
  30.5 1.3 %collective-permute-start.10 = (f32[2,768]{1,0:T(2,128)S(1)}, f32[2,768]{1,0:T(2,128)S(1)}, u32[]{:S(2)}, u32[]{:S(2)}) collective-permute-start(f32[2,768]{1,0:T(2,128)S(1)} %get-tuple-element.55.refs_0_), channel_id=1, source_target_pairs={{0,3},{1,2},{2,1},{3,0},{4,7},{5,6},{6,5},{7,4},{8,11},{9,10},{10,... | collective-permute-start | bytes 18440 | tf_op jit(solution)/shard_map/ppermute | solution.py:421
  31.9 0.4 collective-permute-start.8
  32.2 0.5 %collective-permute-start.9 = (f32[2,768]{1,0:T(2,128)S(1)}, f32[2,768]{1,0:T(2,128)S(1)}, u32[]{:S(2)}, u32[]{:S(2)}) collective-permute-start(f32[2,768]{1,0:T(2,128)S(1)} %get-tuple-element.55.refs_0_), channel_id=1, source_target_pairs={{0,2},{1,3},{2,0},{3,1},{4,6},{5,7},{6,4},{7,5},{8,10},{9,11},{10,... | collective-permute-start | bytes 18440 | tf_op jit(solution)/shard_map/ppermute | solution.py:421
  32.7 3.2 %graph.1.m_ref = f32[96,768]{1,0:T(8,128)S(1)} custom-call(s32[3]{0:T(128)S(1)} %pad_add_fusion.here_ref, bf16[96,224]{1,0:T(8,128)(2,1)S(1)} %get-tuple-element.32.whi_ref, bf16[96,224]{1,0:T(8,128)(2,1)S(1)} %get-tuple-element.33.wlo_ref, f32[96,128]{1,0:T(8,128)S(1)} %get-tuple-element.34.scale_ref, s32[128,128]{1,0:T(8,128)S(1)} %get-tuple-element.35.asked_ref, ...), custom_call_target="tpu_custom_call" | custom-call | flops 1000 | bytes 1000 | tf_op jit(solution)/shard_map/graph/pallas_call | solution.py:326
  35.9 0.0 collective-permute-done.10.refs_3_
  35.9 0.0 collective-permute-done.8.refs_1_
  36.0 0.0 collective-permute-done.9.refs_2_
  36.0 4.9 %smooth.1 = (f32[96,5472]{1,0:T(8,128)}, f32[768,5472]{1,0:T(8,128)S(1)}) custom-call(f32[96,768]{1,0:T(8,128)S(1)} %graph.1.m_ref, f32[768,5472]{1,0:T(8,128)S(1)} %get-tuple-element.53.p_ref, f32[16,768]{1,0:T(8,128)S(1)} %get-tuple-element.54.tile_ref, f32[2,768]{1,0:T(2,128)S(1)} %get-tuple-element.55.refs_0_, ...), custom_call_target="tpu_custom_call", output_to_operand_aliasing={{1}: (1, {})} | custom-call | flops 1000 | bytes 1000 | tf_op jit(solution)/shard_map/smooth/pallas_call | solution.py:363
  (9 shorter events, 0.2 us)
Async XLA Ops:
  0.1 9.9 %copy-start = (bf16[1024,5472]{0,1:T(8,128)(2,1)S(1)}, bf16[1024,5472]{0,1:T(8,128)(2,1)}, u32[]{:S(2)}) copy-start(bf16[1024,5472]{0,1:T(8,128)(2,1)} %param.6) | copy-start | bytes 33619972
  1.9 13.2 %collective-permute-start = (bf16[48,1152]{1,0:T(8,128)(2,1)S(1)}, bf16[48,1152]{1,0:T(8,128)(2,1)S(1)}, u32[]{:S(2)}, u32[]{:S(2)}) collective-permute-start(bf16[48,1152]{1,0:T(8,128)(2,1)S(1)} %get-tuple-element.37), channel_id=1, source_target_pairs={{0,8},{4,12},{8,0},{12,4},{16,24},{20,28},{24,16},{28,20},{1,9},{5... | collective-permute-start | bytes 331784 | tf_op jit(solution)/shard_map/ppermute | solution.py:394
  5.0 11.3 %collective-permute-start.1 = (bf16[48,1152]{1,0:T(8,128)(2,1)S(1)}, bf16[48,1152]{1,0:T(8,128)(2,1)S(1)}, u32[]{:S(2)}, u32[]{:S(2)}) collective-permute-start(bf16[48,1152]{1,0:T(8,128)(2,1)S(1)} %get-tuple-element.37), channel_id=1, source_target_pairs={{0,16},{4,20},{8,24},{12,28},{16,0},{20,4},{24,8},{28,12},{1,17},{... | collective-permute-start | bytes 331784 | tf_op jit(solution)/shard_map/ppermute | solution.py:394
  7.6 8.8 %collective-permute-start.2 = (bf16[48,1152]{1,0:T(8,128)(2,1)S(1)}, bf16[48,1152]{1,0:T(8,128)(2,1)S(1)}, u32[]{:S(2)}, u32[]{:S(2)}) collective-permute-start(bf16[48,1152]{1,0:T(8,128)(2,1)S(1)} %get-tuple-element.37), channel_id=1, source_target_pairs={{0,24},{4,28},{8,16},{12,20},{16,8},{20,12},{24,0},{28,4},{1,25},{... | collective-permute-start | bytes 331784 | tf_op jit(solution)/shard_map/ppermute | solution.py:394
  7.6 8.8 %collective-permute-start.3 = (bf16[48,1152]{1,0:T(8,128)(2,1)S(1)}, bf16[48,1152]{1,0:T(8,128)(2,1)S(1)}, u32[]{:S(2)}, u32[]{:S(2)}) collective-permute-start(bf16[48,1152]{1,0:T(8,128)(2,1)S(1)} %get-tuple-element.37), channel_id=1, source_target_pairs={{0,12},{4,8},{8,4},{12,0},{16,28},{20,24},{24,20},{28,16},{1,13},{... | collective-permute-start | bytes 331784 | tf_op jit(solution)/shard_map/ppermute | solution.py:394
  9.4 6.9 %collective-permute-start.4 = (bf16[48,1152]{1,0:T(8,128)(2,1)S(1)}, bf16[48,1152]{1,0:T(8,128)(2,1)S(1)}, u32[]{:S(2)}, u32[]{:S(2)}) collective-permute-start(bf16[48,1152]{1,0:T(8,128)(2,1)S(1)} %get-tuple-element.37), channel_id=1, source_target_pairs={{0,4},{4,0},{8,12},{12,8},{16,20},{20,16},{24,28},{28,24},{1,5},{5... | collective-permute-start | bytes 331784 | tf_op jit(solution)/shard_map/ppermute | solution.py:394
  16.5 2.0 %collective-permute-start.5 = (bf16[240,1152]{1,0:T(8,128)(2,1)S(1)}, bf16[240,1152]{1,0:T(8,128)(2,1)S(1)}, u32[]{:S(2)}, u32[]{:S(2)}) collective-permute-start(bf16[240,1152]{1,0:T(8,128)(2,1)S(1)} %constant_dynamic-update-slice_fusion), channel_id=1, source_target_pairs={{0,1},{1,0},{2,3},{3,2},{4,5},{5,4},{6,7},{7,6},{8,9},{9,8},{10,11... | collective-permute-start | bytes 1658888 | tf_op jit(solution)/shard_map/ppermute | solution.py:391
  16.6 7.9 %collective-permute-start.6 = (bf16[96,1152]{1,0:T(8,128)(2,1)S(1)}, bf16[96,1152]{1,0:T(8,128)(2,1)S(1)}, u32[]{:S(2)}, u32[]{:S(2)}) collective-permute-start(bf16[96,1152]{1,0:T(8,128)(2,1)S(1)} %pad_maximum_fusion), channel_id=1, source_target_pairs={{0,4},{4,0},{8,12},{12,8},{16,20},{20,16},{24,28},{28,24},{1,5},{5... | collective-permute-start | bytes 663560 | tf_op jit(solution)/shard_map/ppermute | solution.py:394
  24.5 1.5 %collective-permute-start.7 = (bf16[96,1152]{1,0:T(8,128)(2,1)S(1)}, bf16[96,1152]{1,0:T(8,128)(2,1)S(1)}, u32[]{:S(2)}, u32[]{:S(2)}) collective-permute-start(bf16[96,1152]{1,0:T(8,128)(2,1)S(1)} %collective-permute-done.6), channel_id=1, source_target_pairs={{0,1},{1,0},{2,3},{3,2},{4,5},{5,4},{6,7},{7,6},{8,9},{9,8},{10,11... | collective-permute-start | bytes 663560 | tf_op jit(solution)/shard_map/ppermute | solution.py:391
  30.5 5.4 %collective-permute-start.10 = (f32[2,768]{1,0:T(2,128)S(1)}, f32[2,768]{1,0:T(2,128)S(1)}, u32[]{:S(2)}, u32[]{:S(2)}) collective-permute-start(f32[2,768]{1,0:T(2,128)S(1)} %get-tuple-element.55.refs_0_), channel_id=1, source_target_pairs={{0,3},{1,2},{2,1},{3,0},{4,7},{5,6},{6,5},{7,4},{8,11},{9,10},{10,... | collective-permute-start | bytes 18440 | tf_op jit(solution)/shard_map/ppermute | solution.py:421
  31.9 4.1 %collective-permute-start.8 = (f32[2,768]{1,0:T(2,128)S(1)}, f32[2,768]{1,0:T(2,128)S(1)}, u32[]{:S(2)}, u32[]{:S(2)}) collective-permute-start(f32[2,768]{1,0:T(2,128)S(1)} %get-tuple-element.55.refs_0_), channel_id=1, source_target_pairs={{0,1},{1,0},{2,3},{3,2},{4,5},{5,4},{6,7},{7,6},{8,9},{9,8},{10,11... | collective-permute-start | bytes 18440 | tf_op jit(solution)/shard_map/ppermute | solution.py:421
  32.2 3.7 %collective-permute-start.9 = (f32[2,768]{1,0:T(2,128)S(1)}, f32[2,768]{1,0:T(2,128)S(1)}, u32[]{:S(2)}, u32[]{:S(2)}) collective-permute-start(f32[2,768]{1,0:T(2,128)S(1)} %get-tuple-element.55.refs_0_), channel_id=1, source_target_pairs={{0,2},{1,3},{2,0},{3,1},{4,6},{5,7},{6,4},{7,5},{8,10},{9,11},{10,... | collective-permute-start | bytes 18440 | tf_op jit(solution)/shard_map/ppermute | solution.py:421

commit v2 on v1

--- a/solution.py
+++ b/solution.py
@@ -51,7 +51,7 @@
 HBM = pl.BlockSpec(memory_space=pltpu.HBM)
 
 
-def table_kernel(here_ref, requests_hbm, e_hbm, neighbours_hbm, weights_hbm, own_ref, mine_ref, table_ref, near_ref, weight_ref, requests_ref, sems):
+def table_kernel(here_ref, requests_hbm, e_hbm, neighbours_hbm, weights_hbm, mine_ref, out_ref, table_ref, near_ref, weight_ref, requests_ref, sems):
     core, me = here_ref[1], here_ref[2]
     rows, depth = e_hbm.shape
     half = rows // 2
@@ -64,7 +64,6 @@
         (neighbours_hbm, near_ref),
         (weights_hbm, weight_ref),
         (e_hbm.at[pl.ds(start, half), :], mine_ref.at[:, :depth]),
-        (e_hbm, own_ref.at[:, :depth]),
     )
     copies = [pltpu.make_async_copy(src, dst, sems.at[i]) for i, (src, dst) in enumerate(moves)]
     for copy in copies:
@@ -86,10 +85,9 @@
     w2 = weight - w0 - w1
     for i, x in enumerate((block.astype(f32), within.astype(f32), w0, w1, w2)):
         table_ref[i * slots : i * slots + k, :] = x
-    own_ref[:, depth:] = table_ref[...].T.astype(bf16)
-    mine_ref[:, depth:] = own_ref[pl.ds(start, half), depth:]
-    for copy in copies[3:]:
-        copy.wait()
+    out_ref[...] = table_ref[...].T.astype(bf16)
+    mine_ref[:, depth:] = out_ref[pl.ds(start, half), :]
+    copies[3].wait()
 
 
 def tables_of(here, requests, embeddings, neighbours, weights):
@@ -99,13 +97,13 @@
         table_kernel,
         in_specs=[SCALARS] + [HBM] * 4,
         out_specs=[WHOLE] * 2,
-        out_shape=[VMEM((rows, depth + LANES), bf16), VMEM((rows // 2, depth + LANES), bf16)],
+        out_shape=[VMEM((rows // 2, depth + LANES), bf16), VMEM((rows, LANES), bf16)],
         scratch_shapes=[
             VMEM((LANES, rows), f32),
             VMEM((k, rows), jnp.int32),
             VMEM((k, rows), f32),
             pltpu.SMEM(requests.shape, jnp.int32),
-            pltpu.SemaphoreType.DMA((5,)),
+            pltpu.SemaphoreType.DMA((4,)),
         ],
         compiler_params=pltpu.CompilerParams(vmem_limit_bytes=MIB),
         cost_estimate=pl.CostEstimate(flops=3 * 10**10, bytes_accessed=10**8, transcendentals=0),
@@ -208,9 +206,24 @@
     return place + within
 
 
-def own_kernel(tiles, min_live, order, here_ref, own_ref, ct_ref, requests_hbm, near_hbm, weight_hbm, *refs):
-    p_ref, tab_ref, stat_ref, whi_ref, wlo_ref, scale_ref, asked_ref, pick_ref = refs[:8]
-    e_ref, row_ref, near_ref, weight_ref, requests_ref, sems = refs[8:]
+def second_rows(order, rows_here, me, k, tab, itself, total_rows):
+    n, slots = tab.shape[0], round_up(k, 8)
+    within = pltpu.roll(tab, LANES - slots, 1).astype(jnp.int32)
+    weight = pltpu.roll(tab, LANES - 2 * slots, 1) + pltpu.roll(tab, LANES - 3 * slots, 1) + pltpu.roll(tab, LANES - 4 * slots, 1)
+    place = place_of(order, rows_here, me, tab.astype(jnp.int32), within)
+    column = lax.broadcasted_iota(jnp.int32, (n, total_rows), 1)
+    acc = jnp.where(column == itself, 1.0, 0.0)
+    degree = jnp.zeros((n, 1), f32)
+    for i in range(k):
+        w = weight[:, i : i + 1]
+        acc = acc + jnp.where(column == place[:, i : i + 1], SMOOTHING * w, 0.0)
+        degree = degree + w
+    return split(acc * (1.0 / (1.0 + SMOOTHING * degree)))
+
+
+def own_kernel(tiles, min_live, order, here_ref, table_ref, own_ref, ct_ref, requests_hbm, near_hbm, weight_hbm, *refs):
+    p_ref, tab_ref, stat_ref, m_ref, whi_ref, wlo_ref, asked_ref, pick_ref = refs[:8]
+    row_ref, near_ref, weight_ref, requests_ref, sems = refs[8:]
     me = here_ref[2]
     peers, cap = requests_hbm.shape
     k, rows_here = near_hbm.shape
@@ -223,112 +236,94 @@
     copies = [pltpu.make_async_copy(src, dst, sems.at[i]) for i, (src, dst) in enumerate(moves)]
     for copy in copies:
         copy.start()
-    depth = e_ref.shape[1]
-    e_ref[...] = own_ref[:, :depth]
-    tab_ref[:rows_here, :] = own_ref[:, depth:].astype(f32)
+    tab = table_ref[...].astype(f32)
+    tab_ref[:rows_here, :] = tab
     row_ref[...] = jnp.full_like(row_ref, -1)
     for copy in copies:
         copy.wait()
 
-    def edges():
-        lane = lax.broadcasted_iota(jnp.int32, (1, LANES), 1)
-        for p in range(peers):
-            start = place_of(order, rows_here, me, jnp.full((1, 1), p, jnp.int32), 0)
-            row = jnp.full((1, LANES), -1, jnp.int32)
-            for j in range(cap):
-                row = jnp.where(lane == j, requests_ref[p, j], row)
-            row_ref[p : p + 1, :] = jnp.where(row >= 0, row + start, -1)
-        asked = row_ref[...].T
-        column = lax.broadcasted_iota(jnp.int32, (cap, total_rows), 1)
-        for p in range(peers):
-            one = asked[:cap, p : p + 1]
-            asked_ref[p * cap : (p + 1) * cap, :] = jnp.broadcast_to(one, (cap, LANES))
-            pick_ref[p * cap : (p + 1) * cap, :] = jnp.where(column == one, 1.0, 0.0).astype(bf16)
-        near, weight = near_ref[...].T, weight_ref[...].T
-        column = lax.broadcasted_iota(jnp.int32, whi_ref.shape, 1)
-        acc = jnp.zeros(whi_ref.shape, f32)
+    lane = lax.broadcasted_iota(jnp.int32, (1, LANES), 1)
+    for p in range(peers):
+        start = place_of(order, rows_here, me, jnp.full((1, 1), p, jnp.int32), 0)
+        row = jnp.full((1, LANES), -1, jnp.int32)
+        for j in range(cap):
+            row = jnp.where(lane == j, requests_ref[p, j], row)
+        row_ref[p : p + 1, :] = jnp.where(row >= 0, row + start, -1)
+    asked = row_ref[...].T
+    column = lax.broadcasted_iota(jnp.int32, (cap, total_rows), 1)
+    for p in range(peers):
+        one = asked[:cap, p : p + 1]
+        asked_ref[p * cap : (p + 1) * cap, :] = jnp.broadcast_to(one, (cap, LANES))
+        pick_ref[p * cap : (p + 1) * cap, :] = jnp.where(column == one, 1.0, 0.0).astype(bf16)
+
+    near, weight = near_ref[...].T, weight_ref[...].T
+    scale = 1.0 / (1.0 + SMOOTHING * jnp.sum(weight, axis=1, keepdims=True))
+
+    def edges(offset, n):
+        column = lax.broadcasted_iota(jnp.int32, (rows_here, n), 1) + offset
+        acc = jnp.zeros((rows_here, n), f32)
         for i in range(k):
             acc = acc + jnp.where(column == near[:, i : i + 1], SMOOTHING * weight[:, i : i + 1], 0.0)
-        scale = 1.0 / (1.0 + SMOOTHING * jnp.sum(weight, axis=1, keepdims=True))
-        whi_ref[...], wlo_ref[...] = split(acc * scale)
-        scale_ref[...] = jnp.broadcast_to(scale, scale_ref.shape)
-
-    edges()
-    add_powers(tiles, min_live, here_ref, e_ref, ct_ref, p_ref, slice(0, rows_here), stat_ref)
-
-
-def own_powers(here, own, requests, neighbours, weights, classes, order, total_rows, min_live):
-    rows_here = own.shape[0]
-    width, depth = classes.shape
-    k = neighbours.shape[1]
-    extended = rows_here + requests.size
+        return split(acc * scale)
+
+    whi_ref[...], wlo_ref[...] = edges(rows_here, whi_ref.shape[1])
+    whi, wlo = edges(0, rows_here)
+    itself = lax.broadcasted_iota(jnp.int32, (rows_here, 1), 0)
+    thi, tlo = second_rows(order, rows_here, me, k, tab, itself, total_rows)
+    own = jnp.where(lax.broadcasted_iota(jnp.int32, (rows_here, total_rows), 1) == itself, scale, 0.0)
+    m_ref[...] = own + dot(whi, thi) + dot(wlo, thi) + dot(whi, tlo)
+    add_powers(tiles, min_live, here_ref, own_ref, ct_ref, p_ref, slice(0, rows_here), stat_ref)
+
+
+def own_powers(here, table, embeddings, requests, neighbours, weights, classes, order, total_rows, min_live):
+    rows_here, k = neighbours.shape
+    width = classes.shape[0]
     tiles = column_tiles(width)
     shapes = powers_shapes(total_rows, width) + [
-        VMEM((rows_here, extended), bf16),
-        VMEM((rows_here, extended), bf16),
-        VMEM((rows_here, LANES), f32),
+        VMEM((rows_here, total_rows), f32),
+        VMEM((rows_here, requests.size), bf16),
+        VMEM((rows_here, requests.size), bf16),
         VMEM((requests.size, LANES), jnp.int32),
         VMEM((requests.size, total_rows), bf16),
     ]
     return pl.pallas_call(
         functools.partial(own_kernel, tiles, min_live, order),
-        in_specs=[SCALARS, WHOLE, WHOLE] + [HBM] * 3,
+        in_specs=[SCALARS] + [WHOLE] * 3 + [HBM] * 3,
         out_specs=[WHOLE] * len(shapes),
         out_shape=shapes,
         scratch_shapes=[
-            VMEM((rows_here, depth), bf16),
             VMEM((LANES, LANES), jnp.int32),
             VMEM((k, rows_here), jnp.int32),
             VMEM((k, rows_here), f32),
             pltpu.SMEM(requests.shape, jnp.int32),
             pltpu.SemaphoreType.DMA((3,)),
         ],
-        compiler_params=pltpu.CompilerParams(vmem_limit_bytes=8 * MIB),
+        compiler_params=pltpu.CompilerParams(vmem_limit_bytes=(8 if total_rows <= 768 else 14) * MIB),
         cost_estimate=FREE,
         name="own",
-    )(here, resident(own), classes, *[outside(x) for x in (requests, neighbours.T, weights.T)])
-
-
-def spans(rows_here, extended):
-    return [(0, rows_here)] + [(a, min(GROUP, extended - a)) for a in range(rows_here, extended, GROUP)]
-
-
-def graph_kernel(order, k, here_ref, whi_ref, wlo_ref, scale_ref, asked_ref, pick_ref, tab_ref, m_ref, rows_ref, thi_ref, tlo_ref):
-    me = here_ref[2]
-    total_rows = tab_ref.shape[0]
-    rows_here, extended = whi_ref.shape
-    slots = round_up(k, 8)
-    rows_ref[rows_here:, :] = dot(pick_ref[...], tab_ref[...].astype(bf16))
-    for start, size in spans(rows_here, extended):
-        column = lax.broadcasted_iota(jnp.int32, (size, total_rows), 1)
-        tab = tab_ref[:rows_here, :] if start < rows_here else rows_ref[start : start + size, :]
-        within = pltpu.roll(tab, LANES - slots, 1).astype(jnp.int32)
-        weight = pltpu.roll(tab, LANES - 2 * slots, 1) + pltpu.roll(tab, LANES - 3 * slots, 1) + pltpu.roll(tab, LANES - 4 * slots, 1)
-        place = place_of(order, rows_here, me, tab.astype(jnp.int32), within)
-        itself = lax.broadcasted_iota(jnp.int32, (size, LANES), 0) if start < rows_here else asked_ref[start - rows_here : start - rows_here + size, :]
-        acc = jnp.where(column == itself[:, :1], 1.0, 0.0)
-        degree = jnp.zeros((size, 1), f32)
-        for i in range(k):
-            w = weight[:, i : i + 1]
-            acc = acc + jnp.where(column == place[:, i : i + 1], SMOOTHING * w, 0.0)
-            degree = degree + w
-        thi_ref[start : start + size, :], tlo_ref[start : start + size, :] = split(acc * (1.0 / (1.0 + SMOOTHING * degree)))
-    column = lax.broadcasted_iota(jnp.int32, (rows_here, total_rows), 1)
-    sub = lax.broadcasted_iota(jnp.int32, (rows_here, total_rows), 0)
-    own = jnp.where(column == sub, scale_ref[:, :1], 0.0)
-    thi = thi_ref[...]
-    m_ref[...] = own + dot(whi_ref[...], thi) + dot(wlo_ref[...], thi) + dot(whi_ref[...], tlo_ref[...])
+    )(here, resident(table), embeddings, classes, *[outside(x) for x in (requests, neighbours.T, weights.T)])
+
+
+def graph_kernel(order, k, here_ref, m_ref, whi_ref, wlo_ref, asked_ref, pick_ref, tab_ref, out_ref):
+    rows_here, total_rows = m_ref.shape
+    asked = whi_ref.shape[1]
+    tab = dot(pick_ref[...], tab_ref[...].astype(bf16))
+    acc = m_ref[...]
+    for start in range(0, asked, GROUP):
+        rows = slice(start, min(start + GROUP, asked))
+        thi, tlo = second_rows(order, rows_here, here_ref[2], k, tab[rows], asked_ref[rows, :1], total_rows)
+        whi, wlo = whi_ref[:, rows], wlo_ref[:, rows]
+        acc = acc + dot(whi, thi) + dot(wlo, thi) + dot(whi, tlo)
+    out_ref[...] = acc
 
 
 def graph_of(here, edges, tab, order, k):
     total_rows = tab.shape[0]
-    rows_here, extended = edges[0].shape
     return pl.pallas_call(
         functools.partial(graph_kernel, order, k),
         in_specs=[SCALARS] + [WHOLE] * 6,
         out_specs=WHOLE,
-        out_shape=VMEM((rows_here, total_rows), f32),
-        scratch_shapes=[VMEM((extended, LANES), f32), VMEM((extended, total_rows), bf16), VMEM((extended, total_rows), bf16)],
+        out_shape=VMEM(edges[0].shape, f32),
         compiler_params=pltpu.CompilerParams(vmem_limit_bytes=(6 if total_rows <= 768 else 20) * MIB),
         cost_estimate=FREE,
         name="graph",
@@ -338,7 +333,8 @@
 def apply_kernel(tiles, m_ref, p_ref, tile_ref, *refs):
     *stat_refs, out_ref, _, staged, sems = refs
     rows_here = m_ref.shape[0]
-    tops, sums = [r[0:1, :] for r in stat_refs], [r[1:2, :] for r in stat_refs]
+    tops = [r[i : i + 1, :] for r in stat_refs for i in (0, 2)]
+    sums = [r[i : i + 1, :] for r in stat_refs for i in (1, 3)]
     top = functools.reduce(jnp.maximum, tops)
     total = sum(s * jnp.exp(t - top) for s, t in zip(sums, tops))
     factors = jnp.exp(tile_ref[...] - top) / total
@@ -355,11 +351,11 @@
         copy.wait()
 
 
-def applied(m, powers, tile_tops, stats, far):
+def applied(m, powers, tile_tops, stats):
     rows_here, width = m.shape[0], powers.shape[1]
     total_rows = m.shape[1]
     tiles = column_tiles(width)
-    operands = [m, powers, tile_tops, stats, *far]
+    operands = [m, powers, tile_tops, *stats]
     return pl.pallas_call(
         functools.partial(apply_kernel, tiles),
         in_specs=[WHOLE] * len(operands),
@@ -383,7 +379,7 @@
     min_live = min(width, LIVE - (n_cls - 1) * width)
 
     classes = class_text_embedding.T
-    own, mine = tables_of(here, requests[0], embeddings, neighbours, weights)
+    mine, table = tables_of(here, requests[0], embeddings, neighbours, weights)
     first, relayed, beside, last = exchange_plan(n_img)
     order = [0] + [b for piece in beside + last for b in piece]
 
@@ -399,7 +395,7 @@
         return {b: [x[c], other[c]] for b, c in zip(blocks, cuts)}
 
     held = [exchange(mine, b) for b in first]
-    results = own_powers(here, own, requests[0], neighbours, weights, classes, order, total_rows, min_live)
+    results = own_powers(here, table, embeddings, requests[0], neighbours, weights, classes, order, total_rows, min_live)
     buffers, first_row, edges = list(results[:3]), rows_here, results[3:]
 
     def work(blocks):
@@ -418,9 +414,11 @@
     for piece in last:
         work(piece)
     powers, tab, _, tile_tops, stats = buffers
-    far = [lax.ppermute(stats, "cls", [(i, i ^ d) for i in range(n_cls)]) for d in range(1, n_cls)]
+    stats = jnp.concatenate([stats, swap(stats)], axis=0)
+    stats, tab = lax.optimization_barrier((stats, tab))
+    far = [lax.ppermute(stats, "cls", [(i, i ^ d) for i in range(n_cls)]) for d in range(2, n_cls, 2)]
     m = graph_of(here, edges, tab, order, neighbours.shape[1])
-    return applied(m, powers, tile_tops, stats, far)
+    return applied(m, powers, tile_tops, [stats, *far])
 
 
 def solution(mesh):

time: 41.2 us -> 40.9 us (level)
  starting transfers between devices: 11.9 us -> 11.4 us
    pallas_call x1, Pallas kernels: 5.11 us -> 6.39 us  [own_powers(): pl.pallas_call(functools.partial(own_kernel, tiles, min_live, order), in_...]
    ppermute x6, waiting for transfers between devices: 1.55 us -> 0.29 us  [exchange(): return lax.ppermute(x, 'img', [(i, i ^ step) for i in range(n_img)])]
    ppermute x2 -> x3, waiting for transfers between devices: 1.73 us -> 2.81 us  [swap(): return lax.ppermute(x, 'cls', [(i, i ^ 1) for i in range(n_cls)])]
    pallas_call x1, Pallas kernels: 3.21 us -> 2.13 us  [graph_of(): pl.pallas_call(functools.partial(graph_kernel, order, k), in_specs=[SCALA...]
    ppermute x3 -> x1, starting transfers between devices: 2.18 us -> 1.56 us  [shards(): lax.ppermute(stats, 'cls', [(i, i ^ d) for i in range(n_cls)])]
  transfers between devices with their start and end apart: 11 -> 10, of which waited for: 4 -> 5; matrix products, arithmetic and copies ran while one was open for 0% -> 0% of each run, Pallas kernels for 34% -> 35%
where the time goes in v2:
time: 40.9 us; the launch traced here: 40.7 us
  Pallas kernels  25.6 us (63%)
  starting transfers between devices  11.4 us (28%)
  waiting for transfers between devices  3.15 us (8%)
    pallas_call x2, Pallas kernels, powers_of(): pl.pallas_call(functools.partial(powers_kernel, tiles, min_live, depth, f...  10.4 us
    ppermute x6, starting transfers between devices, exchange(): return lax.ppermute(x, 'img', [(i, i ^ step) for i in range(n_img)])  9.63 us
    pallas_call x1, Pallas kernels, own_powers(): pl.pallas_call(functools.partial(own_kernel, tiles, min_live, order), in_...  6.39 us
    pallas_call x1, Pallas kernels, applied(): pl.pallas_call(functools.partial(apply_kernel, tiles), in_specs=[WHOLE] *...  4.89 us
    ppermute x3, waiting for transfers between devices, swap(): return lax.ppermute(x, 'cls', [(i, i ^ 1) for i in range(n_cls)])  2.81 us
    pallas_call x1, Pallas kernels, graph_of(): pl.pallas_call(functools.partial(graph_kernel, order, k), in_specs=[SCALA...  2.13 us
    pallas_call x1, Pallas kernels, tables_of(): pl.pallas_call(table_kernel, in_specs=[SCALARS] + [HBM] * 4, out_specs=[W...  1.73 us
    ppermute x1, starting transfers between devices, shards(): lax.ppermute(stats, 'cls', [(i, i ^ d) for i in range(n_cls)])  1.56 us
  transfers between devices with their start and end apart: 10, of which 5 were waited for; matrix products, arithmetic and copies ran while one was open for 0% of the time, Pallas kernels for 35%

profile of v2, /device:TPU:0, one launch (start us, length us, event | category | flops | bytes accessed | tf_op | source)
XLA Modules:
  0.0 40.7 jit_solution(8604211392696534830)
XLA Ops:
  0.0 0.1 pad_add_fusion.here_ref
  0.1 0.0 copy-start
  0.1 0.0 copy-start.1
  0.1 1.7 %tables.1 = (bf16[48,1152]{1,0:T(8,128)(2,1)S(1)}, bf16[96,128]{1,0:T(8,128)(2,1)S(1)}) custom-call(s32[3]{0:T(128)S(1)} %pad_add_fusion.here_ref, s32[8,16]{1,0:T(8,128)} %bitcast.14, bf16[96,1024]{1,0:T(8,128)(2,1)} %own_ref.1, s32[10,96]{1,0:T(8,128)} %bitcast.10, f32[10,96]{1,0:T(8,128)} %bitcast.12), custom_call_target="tpu_custom_call" | custom-call | flops 30000001024 | bytes 100000000 | tf_op jit(solution)/shard_map/tables/pallas_call | solution.py:96
  1.8 3.1 %collective-permute-start = (bf16[48,1152]{1,0:T(8,128)(2,1)S(1)}, bf16[48,1152]{1,0:T(8,128)(2,1)S(1)}, u32[]{:S(2)}, u32[]{:S(2)}) collective-permute-start(bf16[48,1152]{1,0:T(8,128)(2,1)S(1)} %get-tuple-element.39), channel_id=1, source_target_pairs={{0,8},{4,12},{8,0},{12,4},{16,24},{20,28},{24,16},{28,20},{1,9},{5... | collective-permute-start | bytes 331784 | tf_op jit(solution)/shard_map/ppermute | solution.py:390
  4.9 2.6 %collective-permute-start.1 = (bf16[48,1152]{1,0:T(8,128)(2,1)S(1)}, bf16[48,1152]{1,0:T(8,128)(2,1)S(1)}, u32[]{:S(2)}, u32[]{:S(2)}) collective-permute-start(bf16[48,1152]{1,0:T(8,128)(2,1)S(1)} %get-tuple-element.39), channel_id=1, source_target_pairs={{0,16},{4,20},{8,24},{12,28},{16,0},{20,4},{24,8},{28,12},{1,17},{... | collective-permute-start | bytes 331784 | tf_op jit(solution)/shard_map/ppermute | solution.py:390
  7.5 0.0 collective-permute-start.2
  7.5 1.9 %collective-permute-start.3 = (bf16[48,1152]{1,0:T(8,128)(2,1)S(1)}, bf16[48,1152]{1,0:T(8,128)(2,1)S(1)}, u32[]{:S(2)}, u32[]{:S(2)}) collective-permute-start(bf16[48,1152]{1,0:T(8,128)(2,1)S(1)} %get-tuple-element.39), channel_id=1, source_target_pairs={{0,12},{4,8},{8,4},{12,0},{16,28},{20,24},{24,20},{28,16},{1,13},{... | collective-permute-start | bytes 331784 | tf_op jit(solution)/shard_map/ppermute | solution.py:390
  9.4 0.5 %collective-permute-start.4 = (bf16[48,1152]{1,0:T(8,128)(2,1)S(1)}, bf16[48,1152]{1,0:T(8,128)(2,1)S(1)}, u32[]{:S(2)}, u32[]{:S(2)}) collective-permute-start(bf16[48,1152]{1,0:T(8,128)(2,1)S(1)} %get-tuple-element.39), channel_id=1, source_target_pairs={{0,4},{4,0},{8,12},{12,8},{16,20},{20,16},{24,28},{28,24},{1,5},{5... | collective-permute-start | bytes 331784 | tf_op jit(solution)/shard_map/ppermute | solution.py:390
  9.9 0.0 copy-done
  9.9 0.0 copy-done.1
  9.9 6.4 %own.1 = (f32[768,5472]{1,0:T(8,128)S(1)}, f32[768,128]{1,0:T(8,128)S(1)}, f32[768,128]{1,0:T(8,128)S(1)}, f32[96,768]{1,0:T(8,128)S(1)}, bf16[96,128]{1,0:T(8,1...) custom-call(s32[3]{0:T(128)S(1)} %pad_add_fusion.here_ref, ...), custom_call_target="tpu_custom_call" | custom-call | flops 1000 | bytes 1000 | tf_op jit(solution)/shard_map/own/pallas_call | solution.py:289
  16.3 0.0 collective-permute-done.refs_0_
  16.3 0.0 collective-permute-done.1.refs_2_
  16.3 0.0 collective-permute-done.2.refs_4_
  16.3 0.0 collective-permute-done.3.refs_0_
  16.3 0.0 collective-permute-done.4.refs_6_
  16.4 0.1 collective-permute-start.5
  16.5 1.6 %collective-permute-start.6 = (bf16[96,1152]{1,0:T(8,128)(2,1)S(1)}, bf16[96,1152]{1,0:T(8,128)(2,1)S(1)}, u32[]{:S(2)}, u32[]{:S(2)}) collective-permute-start(bf16[96,1152]{1,0:T(8,128)(2,1)S(1)} %pad_maximum_fusion), channel_id=1, source_target_pairs={{0,4},{4,0},{8,12},{12,8},{16,20},{20,16},{24,28},{28,24},{1,5},{5... | collective-permute-start | bytes 663560 | tf_op jit(solution)/shard_map/ppermute | solution.py:390
  18.1 0.3 collective-permute-done.5
  18.5 5.7 %powers.2 = (f32[768,5472]{1,0:T(8,128)S(1)}, f32[768,128]{1,0:T(8,128)S(1)}, f32[768,128]{1,0:T(8,128)S(1)}) custom-call(s32[3]{0:T(128)S(1)} %pad_add_fusion.here_ref, bf16[48,1152]{1,0:T(8,128)(2,1)S(1)} %collective-permute-done.refs_0_, ...), custom_call_target="tpu_custom_call", output_to_operand_aliasing={{0}: (10, {}), {1}: (11, {}), {2}: (12, {})} | custom-call | flops 1000 | bytes 1000 | tf_op jit(solution)/shard_map/powers/pallas_call | solution.py:188
  24.1 0.3 collective-permute-done.6
  24.4 0.0 collective-permute-start.7
  24.4 1.5 %collective-permute-done.7 = bf16[96,1152]{1,0:T(8,128)(2,1)S(1)} collective-permute-done((bf16[96,1152]{1,0:T(8,128)(2,1)S(1)}, bf16[96,1152]{1,0:T(8,128)(2,1)S(1)}, u32[]{:S(2)}, u32[]{:S(2)}) %collective-permute-start.7) | collective-permute-done | bytes 221216 | tf_op jit(solution)/shard_map/ppermute | solution.py:387
  25.9 4.8 %powers.3 = (f32[768,5472]{1,0:T(8,128)S(1)}, f32[768,128]{1,0:T(8,128)S(1)}, f32[768,128]{1,0:T(8,128)S(1)}, f32[16,768]{1,0:T(8,128)S(1)}, f32[2,768]{1,0:T(2,128)S(1)}) custom-call(s32[3]{0:T(128)S(1)} %pad_add_fusion.here_ref, bf16[48,1152]{1,0:T(8,128)(2,1)S(1)} %collective-permute-done.3.refs_0_, ...), custom_call_target="tpu_custom_call", output_to_operand_aliasing={{0}: (8, {}), {1}: (9, {}), {2}: (10, {})} | custom-call | flops 1000 | bytes 1000 | tf_op jit(solution)/shard_map/powers/pallas_call | solution.py:188
  30.7 0.2 collective-permute-start.8
  30.9 1.0 %collective-permute-done.8 = f32[2,768]{1,0:T(2,128)S(1)} collective-permute-done((f32[2,768]{1,0:T(2,128)S(1)}, f32[2,768]{1,0:T(2,128)S(1)}, u32[]{:S(2)}, u32[]{:S(2)}) %collective-permute-start.8) | collective-permute-done | bytes 6176 | tf_op jit(solution)/shard_map/ppermute | solution.py:387
  31.9 1.6 %collective-permute-start.9 = (f32[4,768]{1,0:T(4,128)S(1)}, f32[4,768]{1,0:T(4,128)S(1)}, u32[]{:S(2)}, u32[]{:S(2)}) collective-permute-start(f32[4,768]{1,0:T(4,128)S(1)} %pad_maximum_fusion.1.refs_0_), channel_id=1, source_target_pairs={{0,2},{1,3},{2,0},{3,1},{4,6},{5,7},{6,4},{7,5},{8,10},{9,11},{10,... | collective-permute-start | bytes 36872 | tf_op jit(solution)/shard_map/ppermute | solution.py:419
  33.5 2.1 %graph.1.m_ref = f32[96,768]{1,0:T(8,128)S(1)} custom-call(s32[3]{0:T(128)S(1)} %pad_add_fusion.here_ref, f32[96,768]{1,0:T(8,128)S(1)} %get-tuple-element.34.m_ref, bf16[96,128]{1,0:T(8,128)(2,1)S(1)} %get-tuple-element.35.whi_ref, bf16[96,128]{1,0:T(8,128)(2,1)S(1)} %get-tuple-element.36.wlo_ref, s32[128,128]{1,0:T(8,128)S(1)} %get-tuple-element.37.asked_ref, ...), custom_call_target="tpu_custom_call" | custom-call | flops 1000 | bytes 1000 | tf_op jit(solution)/shard_map/graph/pallas_call | solution.py:322
  35.6 0.1 collective-permute-done.9.refs_1_
  35.7 4.9 %smooth.1 = (f32[96,5472]{1,0:T(8,128)}, f32[768,5472]{1,0:T(8,128)S(1)}) custom-call(f32[96,768]{1,0:T(8,128)S(1)} %graph.1.m_ref, f32[768,5472]{1,0:T(8,128)S(1)} %get-tuple-element.57.p_ref, f32[16,768]{1,0:T(8,128)S(1)} %get-tuple-element.58.tile_ref, f32[4,768]{1,0:T(4,128)S(1)} %pad_maximum_fusion.1.refs_0_, ...), custom_call_target="tpu_custom_call", output_to_operand_aliasing={{1}: (1, {})} | custom-call | flops 1000 | bytes 1000 | tf_op jit(solution)/shard_map/smooth/pallas_call | solution.py:359
  (10 shorter events, 0.2 us)
Async XLA Ops:
  0.1 9.8 %copy-start = (bf16[1024,5472]{0,1:T(8,128)(2,1)S(1)}, bf16[1024,5472]{0,1:T(8,128)(2,1)}, u32[]{:S(2)}) copy-start(bf16[1024,5472]{0,1:T(8,128)(2,1)} %param.6) | copy-start | bytes 33619972
  0.1 9.8 %copy-start.1 = (bf16[96,1024]{1,0:T(8,128)(2,1)S(1)}, bf16[96,1024]{1,0:T(8,128)(2,1)}, u32[]{:S(2)}) copy-start(bf16[96,1024]{1,0:T(8,128)(2,1)} %own_ref.1) | copy-start | bytes 589828
  1.8 14.4 %collective-permute-start = (bf16[48,1152]{1,0:T(8,128)(2,1)S(1)}, bf16[48,1152]{1,0:T(8,128)(2,1)S(1)}, u32[]{:S(2)}, u32[]{:S(2)}) collective-permute-start(bf16[48,1152]{1,0:T(8,128)(2,1)S(1)} %get-tuple-element.39), channel_id=1, source_target_pairs={{0,8},{4,12},{8,0},{12,4},{16,24},{20,28},{24,16},{28,20},{1,9},{5... | collective-permute-start | bytes 331784 | tf_op jit(solution)/shard_map/ppermute | solution.py:390
  4.9 11.4 %collective-permute-start.1 = (bf16[48,1152]{1,0:T(8,128)(2,1)S(1)}, bf16[48,1152]{1,0:T(8,128)(2,1)S(1)}, u32[]{:S(2)}, u32[]{:S(2)}) collective-permute-start(bf16[48,1152]{1,0:T(8,128)(2,1)S(1)} %get-tuple-element.39), channel_id=1, source_target_pairs={{0,16},{4,20},{8,24},{12,28},{16,0},{20,4},{24,8},{28,12},{1,17},{... | collective-permute-start | bytes 331784 | tf_op jit(solution)/shard_map/ppermute | solution.py:390
  7.5 8.8 %collective-permute-start.2 = (bf16[48,1152]{1,0:T(8,128)(2,1)S(1)}, bf16[48,1152]{1,0:T(8,128)(2,1)S(1)}, u32[]{:S(2)}, u32[]{:S(2)}) collective-permute-start(bf16[48,1152]{1,0:T(8,128)(2,1)S(1)} %get-tuple-element.39), channel_id=1, source_target_pairs={{0,24},{4,28},{8,16},{12,20},{16,8},{20,12},{24,0},{28,4},{1,25},{... | collective-permute-start | bytes 331784 | tf_op jit(solution)/shard_map/ppermute | solution.py:390
  7.5 8.8 %collective-permute-start.3 = (bf16[48,1152]{1,0:T(8,128)(2,1)S(1)}, bf16[48,1152]{1,0:T(8,128)(2,1)S(1)}, u32[]{:S(2)}, u32[]{:S(2)}) collective-permute-start(bf16[48,1152]{1,0:T(8,128)(2,1)S(1)} %get-tuple-element.39), channel_id=1, source_target_pairs={{0,12},{4,8},{8,4},{12,0},{16,28},{20,24},{24,20},{28,16},{1,13},{... | collective-permute-start | bytes 331784 | tf_op jit(solution)/shard_map/ppermute | solution.py:390
  9.4 7.0 %collective-permute-start.4 = (bf16[48,1152]{1,0:T(8,128)(2,1)S(1)}, bf16[48,1152]{1,0:T(8,128)(2,1)S(1)}, u32[]{:S(2)}, u32[]{:S(2)}) collective-permute-start(bf16[48,1152]{1,0:T(8,128)(2,1)S(1)} %get-tuple-element.39), channel_id=1, source_target_pairs={{0,4},{4,0},{8,12},{12,8},{16,20},{20,16},{24,28},{28,24},{1,5},{5... | collective-permute-start | bytes 331784 | tf_op jit(solution)/shard_map/ppermute | solution.py:390
  16.4 2.0 %collective-permute-start.5 = (bf16[240,1152]{1,0:T(8,128)(2,1)S(1)}, bf16[240,1152]{1,0:T(8,128)(2,1)S(1)}, u32[]{:S(2)}, u32[]{:S(2)}) collective-permute-start(bf16[240,1152]{1,0:T(8,128)(2,1)S(1)} %constant_dynamic-update-slice_fusion), channel_id=1, source_target_pairs={{0,1},{1,0},{2,3},{3,2},{4,5},{5,4},{6,7},{7,6},{8,9},{9,8},{10,11... | collective-permute-start | bytes 1658888 | tf_op jit(solution)/shard_map/ppermute | solution.py:387
  16.5 7.9 %collective-permute-start.6 = (bf16[96,1152]{1,0:T(8,128)(2,1)S(1)}, bf16[96,1152]{1,0:T(8,128)(2,1)S(1)}, u32[]{:S(2)}, u32[]{:S(2)}) collective-permute-start(bf16[96,1152]{1,0:T(8,128)(2,1)S(1)} %pad_maximum_fusion), channel_id=1, source_target_pairs={{0,4},{4,0},{8,12},{12,8},{16,20},{20,16},{24,28},{28,24},{1,5},{5... | collective-permute-start | bytes 663560 | tf_op jit(solution)/shard_map/ppermute | solution.py:390
  24.4 1.5 %collective-permute-start.7 = (bf16[96,1152]{1,0:T(8,128)(2,1)S(1)}, bf16[96,1152]{1,0:T(8,128)(2,1)S(1)}, u32[]{:S(2)}, u32[]{:S(2)}) collective-permute-start(bf16[96,1152]{1,0:T(8,128)(2,1)S(1)} %collective-permute-done.6), channel_id=1, source_target_pairs={{0,1},{1,0},{2,3},{3,2},{4,5},{5,4},{6,7},{7,6},{8,9},{9,8},{10,11... | collective-permute-start | bytes 663560 | tf_op jit(solution)/shard_map/ppermute | solution.py:387
  30.7 1.2 %collective-permute-start.8 = (f32[2,768]{1,0:T(2,128)S(1)}, f32[2,768]{1,0:T(2,128)S(1)}, u32[]{:S(2)}, u32[]{:S(2)}) collective-permute-start(f32[2,768]{1,0:T(2,128)S(1)} %get-tuple-element.54), channel_id=1, source_target_pairs={{0,1},{1,0},{2,3},{3,2},{4,5},{5,4},{6,7},{7,6},{8,9},{9,8},{10,11... | collective-permute-start | bytes 18440 | tf_op jit(solution)/shard_map/ppermute | solution.py:387
  31.9 3.8 %collective-permute-start.9 = (f32[4,768]{1,0:T(4,128)S(1)}, f32[4,768]{1,0:T(4,128)S(1)}, u32[]{:S(2)}, u32[]{:S(2)}) collective-permute-start(f32[4,768]{1,0:T(4,128)S(1)} %pad_maximum_fusion.1.refs_0_), channel_id=1, source_target_pairs={{0,2},{1,3},{2,0},{3,1},{4,6},{5,7},{6,4},{7,5},{8,10},{9,11},{10,... | collective-permute-start | bytes 36872 | tf_op jit(solution)/shard_map/ppermute | solution.py:419

commit v3 on v2

--- a/solution.py
+++ b/solution.py
@@ -151,11 +151,11 @@
 
 def powers_kernel(tiles, min_live, depth, first_row, n_parts, final, here_ref, *refs):
     parts, ct_ref = refs[:n_parts], refs[n_parts]
-    p_ref, tab_ref, stat_ref, *ends, e_ref = refs[n_parts + 4 :]
+    p_ref, tab_ref, stat_ref, *ends, e_ref = refs[n_parts + (6 if final else 4) :]
     if final:
         tile_ref, both_ref = ends
         slots = tile_ref.shape[0]
-        tops, both = row_stats(stat_ref[:first_row, :], slots)
+        tops, both = refs[n_parts + 4][...], refs[n_parts + 5][...]
     core = here_ref[1]
     row = 0
     for i, part in enumerate(parts):
@@ -175,19 +175,19 @@
     return [VMEM((total_rows, width), f32), VMEM((total_rows, LANES), f32), VMEM((total_rows, LANES), f32)]
 
 
-def powers_of(parts, ct, here, buffers, first_row, min_live):
+def powers_of(parts, ct, here, buffers, first_row, min_live, earlier=()):
     width, depth = ct.shape
     rows = sum(p.shape[0] for p in parts)
     total_rows = buffers[0].shape[0]
     tiles = column_tiles(width)
-    final = first_row + rows == total_rows
+    final = bool(earlier)
     n = len(parts)
     shapes = powers_shapes(total_rows, width)
     if final:
         shapes += [VMEM((round_up(len(tiles), 8), total_rows), f32), VMEM((2, total_rows), f32)]
     return pl.pallas_call(
         functools.partial(powers_kernel, tiles, min_live, depth, first_row, n, final),
-        in_specs=[SCALARS] + [WHOLE] * (n + 4),
+        in_specs=[SCALARS] + [WHOLE] * (n + 4 + len(earlier)),
         out_specs=[WHOLE] * len(shapes),
         out_shape=shapes,
         scratch_shapes=[VMEM((rows, depth), bf16)],
@@ -195,7 +195,23 @@
         compiler_params=pltpu.CompilerParams(vmem_limit_bytes=8 * MIB),
         cost_estimate=FREE,
         name="powers",
-    )(here, *[resident(x) for x in parts], ct, *[resident(x) for x in buffers])
+    )(here, *[resident(x) for x in parts], ct, *[resident(x) for x in (*buffers, *earlier)])
+
+
+def early_kernel(rows, stat_ref, tile_ref, both_ref):
+    tile_ref[...], both_ref[...] = row_stats(stat_ref[:rows, :], tile_ref.shape[0])
+
+
+def early_stats(stat, rows, n_tiles):
+    return pl.pallas_call(
+        functools.partial(early_kernel, rows),
+        in_specs=[WHOLE],
+        out_specs=[WHOLE] * 2,
+        out_shape=[VMEM((round_up(n_tiles, 8), rows), f32), VMEM((2, rows), f32)],
+        compiler_params=pltpu.CompilerParams(vmem_limit_bytes=4 * MIB),
+        cost_estimate=FREE,
+        name="early",
+    )(resident(stat))
 
 
 def place_of(order, rows_here, me, block, within):
@@ -398,10 +414,10 @@
     results = own_powers(here, table, embeddings, requests[0], neighbours, weights, classes, order, total_rows, min_live)
     buffers, first_row, edges = list(results[:3]), rows_here, results[3:]
 
-    def work(blocks):
+    def work(blocks, earlier=()):
         nonlocal buffers, first_row
         parts = [x for b in blocks for x in pairs[b]]
-        buffers = list(powers_of(parts, classes, here, buffers, first_row, min_live))
+        buffers = list(powers_of(parts, classes, here, buffers, first_row, min_live, earlier))
         first_row += len(blocks) * rows_here
 
     *held, buffers[2] = lax.optimization_barrier((*held, buffers[2]))
@@ -411,8 +427,9 @@
         work(piece)
     got, buffers[2] = lax.optimization_barrier((got, buffers[2]))
     pairs |= halves(got, [b ^ 1 for b in relayed])
-    for piece in last:
+    for piece in last[:-1]:
         work(piece)
+    work(last[-1], early_stats(buffers[2], first_row, len(column_tiles(width))))
     powers, tab, _, tile_tops, stats = buffers
     stats = jnp.concatenate([stats, swap(stats)], axis=0)
     stats, tab = lax.optimization_barrier((stats, tab))

time: 40.9 us -> 40.9 us (level)
  no operation moved by 1% of the time
where the time goes in v3:
time: 40.9 us; the launch traced here: 40.8 us
  Pallas kernels  25.7 us (63%)
  starting transfers between devices  11.4 us (28%)
  waiting for transfers between devices  3.06 us (7%)
    pallas_call x2, Pallas kernels, powers_of(): pl.pallas_call(functools.partial(powers_kernel, tiles, min_live, depth, f...  10.4 us
    ppermute x6, starting transfers between devices, exchange(): return lax.ppermute(x, 'img', [(i, i ^ step) for i in range(n_img)])  9.63 us
    pallas_call x1, Pallas kernels, own_powers(): pl.pallas_call(functools.partial(own_kernel, tiles, min_live, order), in_...  6.39 us
    pallas_call x1, Pallas kernels, applied(): pl.pallas_call(functools.partial(apply_kernel, tiles), in_specs=[WHOLE] *...  4.87 us
    ppermute x3, waiting for transfers between devices, swap(): return lax.ppermute(x, 'cls', [(i, i ^ 1) for i in range(n_cls)])  2.68 us
    pallas_call x1, Pallas kernels, graph_of(): pl.pallas_call(functools.partial(graph_kernel, order, k), in_specs=[SCALA...  2.12 us
    pallas_call x1, Pallas kernels, tables_of(): pl.pallas_call(table_kernel, in_specs=[SCALARS] + [HBM] * 4, out_specs=[W...  1.73 us
    ppermute x1, starting transfers between devices, shards(): lax.ppermute(stats, 'cls', [(i, i ^ d) for i in range(n_cls)])  1.55 us
  transfers between devices with their start and end apart: 10, of which 5 were waited for; matrix products, arithmetic and copies ran while one was open for 0% of the time, Pallas kernels for 35%

profile of v3, /device:TPU:0, one launch (start us, length us, event | category | flops | bytes accessed | tf_op | source)
XLA Modules:
  0.0 40.8 jit_solution(15921290751236677461)
XLA Ops:
  0.0 0.1 pad_add_fusion.here_ref
  0.1 0.0 copy-start
  0.1 0.0 copy-start.1
  0.1 1.7 %tables.1 = (bf16[48,1152]{1,0:T(8,128)(2,1)S(1)}, bf16[96,128]{1,0:T(8,128)(2,1)S(1)}) custom-call(s32[3]{0:T(128)S(1)} %pad_add_fusion.here_ref, s32[8,16]{1,0:T(8,128)} %bitcast.14, bf16[96,1024]{1,0:T(8,128)(2,1)} %own_ref.1, s32[10,96]{1,0:T(8,128)} %bitcast.10, f32[10,96]{1,0:T(8,128)} %bitcast.12), custom_call_target="tpu_custom_call" | custom-call | flops 30000001024 | bytes 100000000 | tf_op jit(solution)/shard_map/tables/pallas_call | solution.py:96
  1.8 3.1 %collective-permute-start = (bf16[48,1152]{1,0:T(8,128)(2,1)S(1)}, bf16[48,1152]{1,0:T(8,128)(2,1)S(1)}, u32[]{:S(2)}, u32[]{:S(2)}) collective-permute-start(bf16[48,1152]{1,0:T(8,128)(2,1)S(1)} %get-tuple-element.41), channel_id=1, source_target_pairs={{0,8},{4,12},{8,0},{12,4},{16,24},{20,28},{24,16},{28,20},{1,9},{5... | collective-permute-start | bytes 331784 | tf_op jit(solution)/shard_map/ppermute | solution.py:406
  4.9 2.6 %collective-permute-start.1 = (bf16[48,1152]{1,0:T(8,128)(2,1)S(1)}, bf16[48,1152]{1,0:T(8,128)(2,1)S(1)}, u32[]{:S(2)}, u32[]{:S(2)}) collective-permute-start(bf16[48,1152]{1,0:T(8,128)(2,1)S(1)} %get-tuple-element.41), channel_id=1, source_target_pairs={{0,16},{4,20},{8,24},{12,28},{16,0},{20,4},{24,8},{28,12},{1,17},{... | collective-permute-start | bytes 331784 | tf_op jit(solution)/shard_map/ppermute | solution.py:406
  7.5 0.0 collective-permute-start.2
  7.5 1.9 %collective-permute-start.3 = (bf16[48,1152]{1,0:T(8,128)(2,1)S(1)}, bf16[48,1152]{1,0:T(8,128)(2,1)S(1)}, u32[]{:S(2)}, u32[]{:S(2)}) collective-permute-start(bf16[48,1152]{1,0:T(8,128)(2,1)S(1)} %get-tuple-element.41), channel_id=1, source_target_pairs={{0,12},{4,8},{8,4},{12,0},{16,28},{20,24},{24,20},{28,16},{1,13},{... | collective-permute-start | bytes 331784 | tf_op jit(solution)/shard_map/ppermute | solution.py:406
  9.4 0.5 %collective-permute-start.4 = (bf16[48,1152]{1,0:T(8,128)(2,1)S(1)}, bf16[48,1152]{1,0:T(8,128)(2,1)S(1)}, u32[]{:S(2)}, u32[]{:S(2)}) collective-permute-start(bf16[48,1152]{1,0:T(8,128)(2,1)S(1)} %get-tuple-element.41), channel_id=1, source_target_pairs={{0,4},{4,0},{8,12},{12,8},{16,20},{20,16},{24,28},{28,24},{1,5},{5... | collective-permute-start | bytes 331784 | tf_op jit(solution)/shard_map/ppermute | solution.py:406
  9.9 0.0 copy-done
  9.9 0.0 copy-done.1
  9.9 6.4 %own.1 = (f32[768,5472]{1,0:T(8,128)S(1)}, f32[768,128]{1,0:T(8,128)S(1)}, f32[768,128]{1,0:T(8,128)S(1)}, f32[96,768]{1,0:T(8,128)S(1)}, bf16[96,128]{1,0:T(8,1...) custom-call(s32[3]{0:T(128)S(1)} %pad_add_fusion.here_ref, ...), custom_call_target="tpu_custom_call" | custom-call | flops 1000 | bytes 1000 | tf_op jit(solution)/shard_map/own/pallas_call | solution.py:305
  16.3 0.0 collective-permute-done.refs_0_
  16.3 0.0 collective-permute-done.1.refs_2_
  16.3 0.0 collective-permute-done.2.refs_4_
  16.3 0.0 collective-permute-done.3.refs_0_
  16.3 0.0 collective-permute-done.4.refs_6_
  16.4 0.1 collective-permute-start.5
  16.5 1.6 %collective-permute-start.6 = (bf16[96,1152]{1,0:T(8,128)(2,1)S(1)}, bf16[96,1152]{1,0:T(8,128)(2,1)S(1)}, u32[]{:S(2)}, u32[]{:S(2)}) collective-permute-start(bf16[96,1152]{1,0:T(8,128)(2,1)S(1)} %pad_maximum_fusion), channel_id=1, source_target_pairs={{0,4},{4,0},{8,12},{12,8},{16,20},{20,16},{24,28},{28,24},{1,5},{5... | collective-permute-start | bytes 663560 | tf_op jit(solution)/shard_map/ppermute | solution.py:406
  18.1 0.3 collective-permute-done.5
  18.5 5.6 %powers.2 = (f32[768,5472]{1,0:T(8,128)S(1)}, f32[768,128]{1,0:T(8,128)S(1)}, f32[768,128]{1,0:T(8,128)S(1)}) custom-call(s32[3]{0:T(128)S(1)} %pad_add_fusion.here_ref, bf16[48,1152]{1,0:T(8,128)(2,1)S(1)} %collective-permute-done.refs_0_, ...), custom_call_target="tpu_custom_call", output_to_operand_aliasing={{0}: (10, {}), {1}: (11, {}), {2}: (12, {})} | custom-call | flops 1000 | bytes 1000 | tf_op jit(solution)/shard_map/powers/pallas_call | solution.py:188
  24.1 0.3 collective-permute-done.6
  24.4 0.0 collective-permute-start.7
  24.4 0.1 early.1
  24.6 1.3 %collective-permute-done.7 = bf16[96,1152]{1,0:T(8,128)(2,1)S(1)} collective-permute-done((bf16[96,1152]{1,0:T(8,128)(2,1)S(1)}, bf16[96,1152]{1,0:T(8,128)(2,1)S(1)}, u32[]{:S(2)}, u32[]{:S(2)}) %collective-permute-start.7) | collective-permute-done | bytes 221216 | tf_op jit(solution)/shard_map/ppermute | solution.py:403
  25.9 4.8 %powers.3 = (f32[768,5472]{1,0:T(8,128)S(1)}, f32[768,128]{1,0:T(8,128)S(1)}, f32[768,128]{1,0:T(8,128)S(1)}, f32[16,768]{1,0:T(8,128)S(1)}, f32[2,768]{1,0:T(2,128)S(1)}) custom-call(s32[3]{0:T(128)S(1)} %pad_add_fusion.here_ref, bf16[48,1152]{1,0:T(8,128)(2,1)S(1)} %collective-permute-done.3.refs_0_, ...), custom_call_target="tpu_custom_call", output_to_operand_aliasing={{0}: (8, {}), {1}: (9, {}), {2}: (10, {})} | custom-call | flops 1000 | bytes 1000 | tf_op jit(solution)/shard_map/powers/pallas_call | solution.py:188
  30.7 0.2 collective-permute-start.8
  30.9 1.0 %collective-permute-done.8 = f32[2,768]{1,0:T(2,128)S(1)} collective-permute-done((f32[2,768]{1,0:T(2,128)S(1)}, f32[2,768]{1,0:T(2,128)S(1)}, u32[]{:S(2)}, u32[]{:S(2)}) %collective-permute-start.8) | collective-permute-done | bytes 6176 | tf_op jit(solution)/shard_map/ppermute | solution.py:403
  32.0 1.6 %collective-permute-start.9 = (f32[4,768]{1,0:T(4,128)S(1)}, f32[4,768]{1,0:T(4,128)S(1)}, u32[]{:S(2)}, u32[]{:S(2)}) collective-permute-start(f32[4,768]{1,0:T(4,128)S(1)} %pad_maximum_fusion.1.refs_0_), channel_id=1, source_target_pairs={{0,2},{1,3},{2,0},{3,1},{4,6},{5,7},{6,4},{7,5},{8,10},{9,11},{10,... | collective-permute-start | bytes 36872 | tf_op jit(solution)/shard_map/ppermute | solution.py:436
  33.5 2.1 %graph.1.m_ref = f32[96,768]{1,0:T(8,128)S(1)} custom-call(s32[3]{0:T(128)S(1)} %pad_add_fusion.here_ref, f32[96,768]{1,0:T(8,128)S(1)} %get-tuple-element.36.m_ref, bf16[96,128]{1,0:T(8,128)(2,1)S(1)} %get-tuple-element.37.whi_ref, bf16[96,128]{1,0:T(8,128)(2,1)S(1)} %get-tuple-element.38.wlo_ref, s32[128,128]{1,0:T(8,128)S(1)} %get-tuple-element.39.asked_ref, ...), custom_call_target="tpu_custom_call" | custom-call | flops 1000 | bytes 1000 | tf_op jit(solution)/shard_map/graph/pallas_call | solution.py:338
  35.7 0.1 collective-permute-done.9.refs_1_
  35.7 4.9 %smooth.1 = (f32[96,5472]{1,0:T(8,128)}, f32[768,5472]{1,0:T(8,128)S(1)}) custom-call(f32[96,768]{1,0:T(8,128)S(1)} %graph.1.m_ref, f32[768,5472]{1,0:T(8,128)S(1)} %get-tuple-element.61.p_ref, f32[16,768]{1,0:T(8,128)S(1)} %get-tuple-element.62.tile_ref, f32[4,768]{1,0:T(4,128)S(1)} %pad_maximum_fusion.1.refs_0_, ...), custom_call_target="tpu_custom_call", output_to_operand_aliasing={{1}: (1, {})} | custom-call | flops 1000 | bytes 1000 | tf_op jit(solution)/shard_map/smooth/pallas_call | solution.py:375
  (10 shorter events, 0.2 us)
Async XLA Ops:
  0.1 9.8 %copy-start = (bf16[1024,5472]{0,1:T(8,128)(2,1)S(1)}, bf16[1024,5472]{0,1:T(8,128)(2,1)}, u32[]{:S(2)}) copy-start(bf16[1024,5472]{0,1:T(8,128)(2,1)} %param.6) | copy-start | bytes 33619972
  0.1 9.8 %copy-start.1 = (bf16[96,1024]{1,0:T(8,128)(2,1)S(1)}, bf16[96,1024]{1,0:T(8,128)(2,1)}, u32[]{:S(2)}) copy-start(bf16[96,1024]{1,0:T(8,128)(2,1)} %own_ref.1) | copy-start | bytes 589828
  1.8 14.4 %collective-permute-start = (bf16[48,1152]{1,0:T(8,128)(2,1)S(1)}, bf16[48,1152]{1,0:T(8,128)(2,1)S(1)}, u32[]{:S(2)}, u32[]{:S(2)}) collective-permute-start(bf16[48,1152]{1,0:T(8,128)(2,1)S(1)} %get-tuple-element.41), channel_id=1, source_target_pairs={{0,8},{4,12},{8,0},{12,4},{16,24},{20,28},{24,16},{28,20},{1,9},{5... | collective-permute-start | bytes 331784 | tf_op jit(solution)/shard_map/ppermute | solution.py:406
  4.9 11.4 %collective-permute-start.1 = (bf16[48,1152]{1,0:T(8,128)(2,1)S(1)}, bf16[48,1152]{1,0:T(8,128)(2,1)S(1)}, u32[]{:S(2)}, u32[]{:S(2)}) collective-permute-start(bf16[48,1152]{1,0:T(8,128)(2,1)S(1)} %get-tuple-element.41), channel_id=1, source_target_pairs={{0,16},{4,20},{8,24},{12,28},{16,0},{20,4},{24,8},{28,12},{1,17},{... | collective-permute-start | bytes 331784 | tf_op jit(solution)/shard_map/ppermute | solution.py:406
  7.5 8.8 %collective-permute-start.2 = (bf16[48,1152]{1,0:T(8,128)(2,1)S(1)}, bf16[48,1152]{1,0:T(8,128)(2,1)S(1)}, u32[]{:S(2)}, u32[]{:S(2)}) collective-permute-start(bf16[48,1152]{1,0:T(8,128)(2,1)S(1)} %get-tuple-element.41), channel_id=1, source_target_pairs={{0,24},{4,28},{8,16},{12,20},{16,8},{20,12},{24,0},{28,4},{1,25},{... | collective-permute-start | bytes 331784 | tf_op jit(solution)/shard_map/ppermute | solution.py:406
  7.5 8.8 %collective-permute-start.3 = (bf16[48,1152]{1,0:T(8,128)(2,1)S(1)}, bf16[48,1152]{1,0:T(8,128)(2,1)S(1)}, u32[]{:S(2)}, u32[]{:S(2)}) collective-permute-start(bf16[48,1152]{1,0:T(8,128)(2,1)S(1)} %get-tuple-element.41), channel_id=1, source_target_pairs={{0,12},{4,8},{8,4},{12,0},{16,28},{20,24},{24,20},{28,16},{1,13},{... | collective-permute-start | bytes 331784 | tf_op jit(solution)/shard_map/ppermute | solution.py:406
  9.4 7.0 %collective-permute-start.4 = (bf16[48,1152]{1,0:T(8,128)(2,1)S(1)}, bf16[48,1152]{1,0:T(8,128)(2,1)S(1)}, u32[]{:S(2)}, u32[]{:S(2)}) collective-permute-start(bf16[48,1152]{1,0:T(8,128)(2,1)S(1)} %get-tuple-element.41), channel_id=1, source_target_pairs={{0,4},{4,0},{8,12},{12,8},{16,20},{20,16},{24,28},{28,24},{1,5},{5... | collective-permute-start | bytes 331784 | tf_op jit(solution)/shard_map/ppermute | solution.py:406
  16.4 2.0 %collective-permute-start.5 = (bf16[240,1152]{1,0:T(8,128)(2,1)S(1)}, bf16[240,1152]{1,0:T(8,128)(2,1)S(1)}, u32[]{:S(2)}, u32[]{:S(2)}) collective-permute-start(bf16[240,1152]{1,0:T(8,128)(2,1)S(1)} %constant_dynamic-update-slice_fusion), channel_id=1, source_target_pairs={{0,1},{1,0},{2,3},{3,2},{4,5},{5,4},{6,7},{7,6},{8,9},{9,8},{10,11... | collective-permute-start | bytes 1658888 | tf_op jit(solution)/shard_map/ppermute | solution.py:403
  16.5 7.9 %collective-permute-start.6 = (bf16[96,1152]{1,0:T(8,128)(2,1)S(1)}, bf16[96,1152]{1,0:T(8,128)(2,1)S(1)}, u32[]{:S(2)}, u32[]{:S(2)}) collective-permute-start(bf16[96,1152]{1,0:T(8,128)(2,1)S(1)} %pad_maximum_fusion), channel_id=1, source_target_pairs={{0,4},{4,0},{8,12},{12,8},{16,20},{20,16},{24,28},{28,24},{1,5},{5... | collective-permute-start | bytes 663560 | tf_op jit(solution)/shard_map/ppermute | solution.py:406
  24.4 1.5 %collective-permute-start.7 = (bf16[96,1152]{1,0:T(8,128)(2,1)S(1)}, bf16[96,1152]{1,0:T(8,128)(2,1)S(1)}, u32[]{:S(2)}, u32[]{:S(2)}) collective-permute-start(bf16[96,1152]{1,0:T(8,128)(2,1)S(1)} %collective-permute-done.6), channel_id=1, source_target_pairs={{0,1},{1,0},{2,3},{3,2},{4,5},{5,4},{6,7},{7,6},{8,9},{9,8},{10,11... | collective-permute-start | bytes 663560 | tf_op jit(solution)/shard_map/ppermute | solution.py:403
  30.7 1.2 %collective-permute-start.8 = (f32[2,768]{1,0:T(2,128)S(1)}, f32[2,768]{1,0:T(2,128)S(1)}, u32[]{:S(2)}, u32[]{:S(2)}) collective-permute-start(f32[2,768]{1,0:T(2,128)S(1)} %get-tuple-element.58), channel_id=1, source_target_pairs={{0,1},{1,0},{2,3},{3,2},{4,5},{5,4},{6,7},{7,6},{8,9},{9,8},{10,11... | collective-permute-start | bytes 18440 | tf_op jit(solution)/shard_map/ppermute | solution.py:403
  32.0 3.8 %collective-permute-start.9 = (f32[4,768]{1,0:T(4,128)S(1)}, f32[4,768]{1,0:T(4,128)S(1)}, u32[]{:S(2)}, u32[]{:S(2)}) collective-permute-start(f32[4,768]{1,0:T(4,128)S(1)} %pad_maximum_fusion.1.refs_0_), channel_id=1, source_target_pairs={{0,2},{1,3},{2,0},{3,1},{4,6},{5,7},{6,4},{7,5},{8,10},{9,11},{10,... | collective-permute-start | bytes 36872 | tf_op jit(solution)/shard_map/ppermute | solution.py:436

commit v4 on v2

--- a/solution.py
+++ b/solution.py
@@ -221,26 +221,16 @@
     return split(acc * (1.0 / (1.0 + SMOOTHING * degree)))
 
 
-def own_kernel(tiles, min_live, order, here_ref, table_ref, own_ref, ct_ref, requests_hbm, near_hbm, weight_hbm, *refs):
+def own_kernel(tiles, min_live, order, here_ref, requests_ref, table_ref, own_ref, ct_ref, near_ref, weight_ref, *refs):
     p_ref, tab_ref, stat_ref, m_ref, whi_ref, wlo_ref, asked_ref, pick_ref = refs[:8]
-    row_ref, near_ref, weight_ref, requests_ref, sems = refs[8:]
+    row_ref = refs[8]
     me = here_ref[2]
-    peers, cap = requests_hbm.shape
-    k, rows_here = near_hbm.shape
+    peers, cap = requests_ref.shape
+    k, rows_here = near_ref.shape
     total_rows = tab_ref.shape[0]
-    moves = (
-        (requests_hbm, requests_ref),
-        (near_hbm, near_ref),
-        (weight_hbm, weight_ref),
-    )
-    copies = [pltpu.make_async_copy(src, dst, sems.at[i]) for i, (src, dst) in enumerate(moves)]
-    for copy in copies:
-        copy.start()
     tab = table_ref[...].astype(f32)
     tab_ref[:rows_here, :] = tab
     row_ref[...] = jnp.full_like(row_ref, -1)
-    for copy in copies:
-        copy.wait()
 
     lane = lax.broadcasted_iota(jnp.int32, (1, LANES), 1)
     for p in range(peers):
@@ -288,20 +278,16 @@
     ]
     return pl.pallas_call(
         functools.partial(own_kernel, tiles, min_live, order),
-        in_specs=[SCALARS] + [WHOLE] * 3 + [HBM] * 3,
+        in_specs=[SCALARS, SCALARS] + [WHOLE] * 5,
         out_specs=[WHOLE] * len(shapes),
         out_shape=shapes,
         scratch_shapes=[
             VMEM((LANES, LANES), jnp.int32),
-            VMEM((k, rows_here), jnp.int32),
-            VMEM((k, rows_here), f32),
-            pltpu.SMEM(requests.shape, jnp.int32),
-            pltpu.SemaphoreType.DMA((3,)),
         ],
         compiler_params=pltpu.CompilerParams(vmem_limit_bytes=(8 if total_rows <= 768 else 14) * MIB),
         cost_estimate=FREE,
         name="own",
-    )(here, resident(table), embeddings, classes, *[outside(x) for x in (requests, neighbours.T, weights.T)])
+    )(here, requests, resident(table), embeddings, classes, neighbours.T, weights.T)
 
 
 def graph_kernel(order, k, here_ref, m_ref, whi_ref, wlo_ref, asked_ref, pick_ref, tab_ref, out_ref):

time: 40.9 us -> 40.8 us (level)
  Pallas kernels: 25.6 us -> 24.9 us
  waiting for transfers between devices: 3.15 us -> 3.69 us
    pallas_call x1, Pallas kernels: 6.39 us -> 5.73 us  [own_powers(): pl.pallas_call(functools.partial(own_kernel, tiles, min_live, order), in_...]
    ppermute x6, waiting for transfers between devices: 0.29 us -> 0.91 us  [exchange(): return lax.ppermute(x, 'img', [(i, i ^ step) for i in range(n_img)])]
  transfers between devices with their start and end apart: 10 -> 10, of which waited for: 5 -> 5; matrix products, arithmetic and copies ran while one was open for 0% -> 0% of each run, Pallas kernels for 35% -> 33%
where the time goes in v4:
time: 40.8 us; the launch traced here: 40.7 us
  Pallas kernels  24.9 us (61%)
  starting transfers between devices  11.5 us (28%)
  waiting for transfers between devices  3.69 us (9%)
    pallas_call x2, Pallas kernels, powers_of(): pl.pallas_call(functools.partial(powers_kernel, tiles, min_live, depth, f...  10.4 us
    ppermute x6, starting transfers between devices, exchange(): return lax.ppermute(x, 'img', [(i, i ^ step) for i in range(n_img)])  9.67 us
    pallas_call x1, Pallas kernels, own_powers(): pl.pallas_call(functools.partial(own_kernel, tiles, min_live, order), in_...  5.73 us
    pallas_call x1, Pallas kernels, applied(): pl.pallas_call(functools.partial(apply_kernel, tiles), in_specs=[WHOLE] *...  4.87 us
    ppermute x3, waiting for transfers between devices, swap(): return lax.ppermute(x, 'cls', [(i, i ^ 1) for i in range(n_cls)])  2.76 us
    pallas_call x1, Pallas kernels, graph_of(): pl.pallas_call(functools.partial(graph_kernel, order, k), in_specs=[SCALA...  2.12 us
    pallas_call x1, Pallas kernels, tables_of(): pl.pallas_call(table_kernel, in_specs=[SCALARS] + [HBM] * 4, out_specs=[W...  1.74 us
    ppermute x1, starting transfers between devices, shards(): lax.ppermute(stats, 'cls', [(i, i ^ d) for i in range(n_cls)])  1.61 us
  transfers between devices with their start and end apart: 10, of which 5 were waited for; matrix products, arithmetic and copies ran while one was open for 0% of the time, Pallas kernels for 33%

profile of v4, /device:TPU:0, one launch (start us, length us, event | category | flops | bytes accessed | tf_op | source)
XLA Modules:
  0.0 40.7 jit_solution(4069980767112606080)
XLA Ops:
  0.0 0.1 pad_add_fusion.here_ref
  0.1 0.0 copy-start
  0.1 0.0 copy-start.1
  0.1 0.0 copy-start.2
  0.1 0.0 copy-start.3
  0.1 0.0 copy-start.4
  0.1 1.7 %tables.1 = (bf16[48,1152]{1,0:T(8,128)(2,1)S(1)}, bf16[96,128]{1,0:T(8,128)(2,1)S(1)}) custom-call(s32[3]{0:T(128)S(1)} %pad_add_fusion.here_ref, s32[8,16]{1,0:T(8,128)} %bitcast.14, bf16[96,1024]{1,0:T(8,128)(2,1)} %own_ref.1, s32[10,96]{1,0:T(8,128)} %bitcast.10, f32[10,96]{1,0:T(8,128)} %bitcast.12), custom_call_target="tpu_custom_call" | custom-call | flops 30000001024 | bytes 100000000 | tf_op jit(solution)/shard_map/tables/pallas_call | solution.py:96
  1.8 3.1 %collective-permute-start = (bf16[48,1152]{1,0:T(8,128)(2,1)S(1)}, bf16[48,1152]{1,0:T(8,128)(2,1)S(1)}, u32[]{:S(2)}, u32[]{:S(2)}) collective-permute-start(bf16[48,1152]{1,0:T(8,128)(2,1)S(1)} %get-tuple-element.39), channel_id=1, source_target_pairs={{0,8},{4,12},{8,0},{12,4},{16,24},{20,28},{24,16},{28,20},{1,9},{5... | collective-permute-start | bytes 331784 | tf_op jit(solution)/shard_map/ppermute | solution.py:376
  4.9 2.6 %collective-permute-start.1 = (bf16[48,1152]{1,0:T(8,128)(2,1)S(1)}, bf16[48,1152]{1,0:T(8,128)(2,1)S(1)}, u32[]{:S(2)}, u32[]{:S(2)}) collective-permute-start(bf16[48,1152]{1,0:T(8,128)(2,1)S(1)} %get-tuple-element.39), channel_id=1, source_target_pairs={{0,16},{4,20},{8,24},{12,28},{16,0},{20,4},{24,8},{28,12},{1,17},{... | collective-permute-start | bytes 331784 | tf_op jit(solution)/shard_map/ppermute | solution.py:376
  7.5 0.0 collective-permute-start.2
  7.5 1.9 %collective-permute-start.3 = (bf16[48,1152]{1,0:T(8,128)(2,1)S(1)}, bf16[48,1152]{1,0:T(8,128)(2,1)S(1)}, u32[]{:S(2)}, u32[]{:S(2)}) collective-permute-start(bf16[48,1152]{1,0:T(8,128)(2,1)S(1)} %get-tuple-element.39), channel_id=1, source_target_pairs={{0,12},{4,8},{8,4},{12,0},{16,28},{20,24},{24,20},{28,16},{1,13},{... | collective-permute-start | bytes 331784 | tf_op jit(solution)/shard_map/ppermute | solution.py:376
  9.4 0.5 %collective-permute-start.4 = (bf16[48,1152]{1,0:T(8,128)(2,1)S(1)}, bf16[48,1152]{1,0:T(8,128)(2,1)S(1)}, u32[]{:S(2)}, u32[]{:S(2)}) collective-permute-start(bf16[48,1152]{1,0:T(8,128)(2,1)S(1)} %get-tuple-element.39), channel_id=1, source_target_pairs={{0,4},{4,0},{8,12},{12,8},{16,20},{20,16},{24,28},{28,24},{1,5},{5... | collective-permute-start | bytes 331784 | tf_op jit(solution)/shard_map/ppermute | solution.py:376
  9.9 0.0 copy-done
  9.9 0.0 copy-done.1
  9.9 0.0 copy-done.2
  9.9 0.0 copy-done.3
  9.9 0.0 copy-done.4
  9.9 5.7 %own.1 = (f32[768,5472]{1,0:T(8,128)S(1)}, f32[768,128]{1,0:T(8,128)S(1)}, f32[768,128]{1,0:T(8,128)S(1)}, f32[96,768]{1,0:T(8,128)S(1)}, bf16[96,128]{1,0:T(8,1...) custom-call(s32[3]{0:T(128)S(1)} %pad_add_fusion.here_ref, ...), custom_call_target="tpu_custom_call" | custom-call | flops 1000 | bytes 1000 | tf_op jit(solution)/shard_map/own/pallas_call | solution.py:279
  15.6 0.0 collective-permute-done.refs_0_
  15.7 0.6 %collective-permute-done.1.refs_2_ = bf16[48,1152]{1,0:T(8,128)(2,1)S(1)} collective-permute-done((bf16[48,1152]{1,0:T(8,128)(2,1)S(1)}, bf16[48,1152]{1,0:T(8,128)(2,1)S(1)}, u32[]{:S(2)}, u32[]{:S(2)}) %collective-permute-start.1) | collective-permute-done | bytes 110624 | tf_op jit(solution)/shard_map/ppermute | solution.py:376
  16.3 0.0 collective-permute-done.2.refs_4_
  16.3 0.0 collective-permute-done.3.refs_0_
  16.3 0.0 collective-permute-done.4.refs_6_
  16.4 0.1 collective-permute-start.5
  16.5 1.6 %collective-permute-start.6 = (bf16[96,1152]{1,0:T(8,128)(2,1)S(1)}, bf16[96,1152]{1,0:T(8,128)(2,1)S(1)}, u32[]{:S(2)}, u32[]{:S(2)}) collective-permute-start(bf16[96,1152]{1,0:T(8,128)(2,1)S(1)} %pad_maximum_fusion), channel_id=1, source_target_pairs={{0,4},{4,0},{8,12},{12,8},{16,20},{20,16},{24,28},{28,24},{1,5},{5... | collective-permute-start | bytes 663560 | tf_op jit(solution)/shard_map/ppermute | solution.py:376
  18.1 0.3 collective-permute-done.5
  18.5 5.7 %powers.2 = (f32[768,5472]{1,0:T(8,128)S(1)}, f32[768,128]{1,0:T(8,128)S(1)}, f32[768,128]{1,0:T(8,128)S(1)}) custom-call(s32[3]{0:T(128)S(1)} %pad_add_fusion.here_ref, bf16[48,1152]{1,0:T(8,128)(2,1)S(1)} %collective-permute-done.refs_0_, ...), custom_call_target="tpu_custom_call", output_to_operand_aliasing={{0}: (10, {}), {1}: (11, {}), {2}: (12, {})} | custom-call | flops 1000 | bytes 1000 | tf_op jit(solution)/shard_map/powers/pallas_call | solution.py:188
  24.1 0.3 collective-permute-done.6
  24.4 0.0 collective-permute-start.7
  24.4 1.5 %collective-permute-done.7 = bf16[96,1152]{1,0:T(8,128)(2,1)S(1)} collective-permute-done((bf16[96,1152]{1,0:T(8,128)(2,1)S(1)}, bf16[96,1152]{1,0:T(8,128)(2,1)S(1)}, u32[]{:S(2)}, u32[]{:S(2)}) %collective-permute-start.7) | collective-permute-done | bytes 221216 | tf_op jit(solution)/shard_map/ppermute | solution.py:373
  25.9 4.8 %powers.3 = (f32[768,5472]{1,0:T(8,128)S(1)}, f32[768,128]{1,0:T(8,128)S(1)}, f32[768,128]{1,0:T(8,128)S(1)}, f32[16,768]{1,0:T(8,128)S(1)}, f32[2,768]{1,0:T(2,128)S(1)}) custom-call(s32[3]{0:T(128)S(1)} %pad_add_fusion.here_ref, bf16[48,1152]{1,0:T(8,128)(2,1)S(1)} %collective-permute-done.3.refs_0_, ...), custom_call_target="tpu_custom_call", output_to_operand_aliasing={{0}: (8, {}), {1}: (9, {}), {2}: (10, {})} | custom-call | flops 1000 | bytes 1000 | tf_op jit(solution)/shard_map/powers/pallas_call | solution.py:188
  30.7 0.2 collective-permute-start.8
  30.9 1.0 %collective-permute-done.8 = f32[2,768]{1,0:T(2,128)S(1)} collective-permute-done((f32[2,768]{1,0:T(2,128)S(1)}, f32[2,768]{1,0:T(2,128)S(1)}, u32[]{:S(2)}, u32[]{:S(2)}) %collective-permute-start.8) | collective-permute-done | bytes 6176 | tf_op jit(solution)/shard_map/ppermute | solution.py:373
  31.9 1.6 %collective-permute-start.9 = (f32[4,768]{1,0:T(4,128)S(1)}, f32[4,768]{1,0:T(4,128)S(1)}, u32[]{:S(2)}, u32[]{:S(2)}) collective-permute-start(f32[4,768]{1,0:T(4,128)S(1)} %pad_maximum_fusion.1.refs_0_), channel_id=1, source_target_pairs={{0,2},{1,3},{2,0},{3,1},{4,6},{5,7},{6,4},{7,5},{8,10},{9,11},{10,... | collective-permute-start | bytes 36872 | tf_op jit(solution)/shard_map/ppermute | solution.py:405
  33.5 2.1 %graph.1.m_ref = f32[96,768]{1,0:T(8,128)S(1)} custom-call(s32[3]{0:T(128)S(1)} %pad_add_fusion.here_ref, f32[96,768]{1,0:T(8,128)S(1)} %get-tuple-element.34.m_ref, bf16[96,128]{1,0:T(8,128)(2,1)S(1)} %get-tuple-element.35.whi_ref, bf16[96,128]{1,0:T(8,128)(2,1)S(1)} %get-tuple-element.36.wlo_ref, s32[128,128]{1,0:T(8,128)S(1)} %get-tuple-element.37.asked_ref, ...), custom_call_target="tpu_custom_call" | custom-call | flops 1000 | bytes 1000 | tf_op jit(solution)/shard_map/graph/pallas_call | solution.py:308
  35.6 0.0 collective-permute-done.9.refs_1_
  35.7 4.9 %smooth.1 = (f32[96,5472]{1,0:T(8,128)}, f32[768,5472]{1,0:T(8,128)S(1)}) custom-call(f32[96,768]{1,0:T(8,128)S(1)} %graph.1.m_ref, f32[768,5472]{1,0:T(8,128)S(1)} %get-tuple-element.57.p_ref, f32[16,768]{1,0:T(8,128)S(1)} %get-tuple-element.58.tile_ref, f32[4,768]{1,0:T(4,128)S(1)} %pad_maximum_fusion.1.refs_0_, ...), custom_call_target="tpu_custom_call", output_to_operand_aliasing={{1}: (1, {})} | custom-call | flops 1000 | bytes 1000 | tf_op jit(solution)/shard_map/smooth/pallas_call | solution.py:345
  (10 shorter events, 0.2 us)
Async XLA Ops:
  0.1 9.8 %copy-start = (bf16[1024,5472]{0,1:T(8,128)(2,1)S(1)}, bf16[1024,5472]{0,1:T(8,128)(2,1)}, u32[]{:S(2)}) copy-start(bf16[1024,5472]{0,1:T(8,128)(2,1)} %param.6) | copy-start | bytes 33619972
  0.1 9.8 %copy-start.1 = (bf16[96,1024]{1,0:T(8,128)(2,1)S(1)}, bf16[96,1024]{1,0:T(8,128)(2,1)}, u32[]{:S(2)}) copy-start(bf16[96,1024]{1,0:T(8,128)(2,1)} %own_ref.1) | copy-start | bytes 589828
  0.1 9.8 %copy-start.2 = (s32[96,10]{0,1:T(8,128)S(1)}, s32[96,10]{0,1:T(8,128)}, u32[]{:S(2)}) copy-start(s32[96,10]{0,1:T(8,128)} %param.7) | copy-start | bytes 11524
  0.1 9.8 %copy-start.3 = (f32[96,10]{0,1:T(8,128)S(1)}, f32[96,10]{0,1:T(8,128)}, u32[]{:S(2)}) copy-start(f32[96,10]{0,1:T(8,128)} %param.8) | copy-start | bytes 11524
  0.1 9.8 %copy-start.4 = (s32[1,8,16]{2,1,0:T(8,128)S(1)}, s32[1,8,16]{2,1,0:T(8,128)}, u32[]{:S(2)}) copy-start(s32[1,8,16]{2,1,0:T(8,128)} %param.9) | copy-start | bytes 1540
  1.8 13.8 %collective-permute-start = (bf16[48,1152]{1,0:T(8,128)(2,1)S(1)}, bf16[48,1152]{1,0:T(8,128)(2,1)S(1)}, u32[]{:S(2)}, u32[]{:S(2)}) collective-permute-start(bf16[48,1152]{1,0:T(8,128)(2,1)S(1)} %get-tuple-element.39), channel_id=1, source_target_pairs={{0,8},{4,12},{8,0},{12,4},{16,24},{20,28},{24,16},{28,20},{1,9},{5... | collective-permute-start | bytes 331784 | tf_op jit(solution)/shard_map/ppermute | solution.py:376
  4.9 11.3 %collective-permute-start.1 = (bf16[48,1152]{1,0:T(8,128)(2,1)S(1)}, bf16[48,1152]{1,0:T(8,128)(2,1)S(1)}, u32[]{:S(2)}, u32[]{:S(2)}) collective-permute-start(bf16[48,1152]{1,0:T(8,128)(2,1)S(1)} %get-tuple-element.39), channel_id=1, source_target_pairs={{0,16},{4,20},{8,24},{12,28},{16,0},{20,4},{24,8},{28,12},{1,17},{... | collective-permute-start | bytes 331784 | tf_op jit(solution)/shard_map/ppermute | solution.py:376
  7.5 8.8 %collective-permute-start.2 = (bf16[48,1152]{1,0:T(8,128)(2,1)S(1)}, bf16[48,1152]{1,0:T(8,128)(2,1)S(1)}, u32[]{:S(2)}, u32[]{:S(2)}) collective-permute-start(bf16[48,1152]{1,0:T(8,128)(2,1)S(1)} %get-tuple-element.39), channel_id=1, source_target_pairs={{0,24},{4,28},{8,16},{12,20},{16,8},{20,12},{24,0},{28,4},{1,25},{... | collective-permute-start | bytes 331784 | tf_op jit(solution)/shard_map/ppermute | solution.py:376
  7.5 8.8 %collective-permute-start.3 = (bf16[48,1152]{1,0:T(8,128)(2,1)S(1)}, bf16[48,1152]{1,0:T(8,128)(2,1)S(1)}, u32[]{:S(2)}, u32[]{:S(2)}) collective-permute-start(bf16[48,1152]{1,0:T(8,128)(2,1)S(1)} %get-tuple-element.39), channel_id=1, source_target_pairs={{0,12},{4,8},{8,4},{12,0},{16,28},{20,24},{24,20},{28,16},{1,13},{... | collective-permute-start | bytes 331784 | tf_op jit(solution)/shard_map/ppermute | solution.py:376
  9.4 6.9 %collective-permute-start.4 = (bf16[48,1152]{1,0:T(8,128)(2,1)S(1)}, bf16[48,1152]{1,0:T(8,128)(2,1)S(1)}, u32[]{:S(2)}, u32[]{:S(2)}) collective-permute-start(bf16[48,1152]{1,0:T(8,128)(2,1)S(1)} %get-tuple-element.39), channel_id=1, source_target_pairs={{0,4},{4,0},{8,12},{12,8},{16,20},{20,16},{24,28},{28,24},{1,5},{5... | collective-permute-start | bytes 331784 | tf_op jit(solution)/shard_map/ppermute | solution.py:376
  16.4 2.0 %collective-permute-start.5 = (bf16[240,1152]{1,0:T(8,128)(2,1)S(1)}, bf16[240,1152]{1,0:T(8,128)(2,1)S(1)}, u32[]{:S(2)}, u32[]{:S(2)}) collective-permute-start(bf16[240,1152]{1,0:T(8,128)(2,1)S(1)} %constant_dynamic-update-slice_fusion), channel_id=1, source_target_pairs={{0,1},{1,0},{2,3},{3,2},{4,5},{5,4},{6,7},{7,6},{8,9},{9,8},{10,11... | collective-permute-start | bytes 1658888 | tf_op jit(solution)/shard_map/ppermute | solution.py:373
  16.5 7.9 %collective-permute-start.6 = (bf16[96,1152]{1,0:T(8,128)(2,1)S(1)}, bf16[96,1152]{1,0:T(8,128)(2,1)S(1)}, u32[]{:S(2)}, u32[]{:S(2)}) collective-permute-start(bf16[96,1152]{1,0:T(8,128)(2,1)S(1)} %pad_maximum_fusion), channel_id=1, source_target_pairs={{0,4},{4,0},{8,12},{12,8},{16,20},{20,16},{24,28},{28,24},{1,5},{5... | collective-permute-start | bytes 663560 | tf_op jit(solution)/shard_map/ppermute | solution.py:376
  24.4 1.5 %collective-permute-start.7 = (bf16[96,1152]{1,0:T(8,128)(2,1)S(1)}, bf16[96,1152]{1,0:T(8,128)(2,1)S(1)}, u32[]{:S(2)}, u32[]{:S(2)}) collective-permute-start(bf16[96,1152]{1,0:T(8,128)(2,1)S(1)} %collective-permute-done.6), channel_id=1, source_target_pairs={{0,1},{1,0},{2,3},{3,2},{4,5},{5,4},{6,7},{7,6},{8,9},{9,8},{10,11... | collective-permute-start | bytes 663560 | tf_op jit(solution)/shard_map/ppermute | solution.py:373
  30.7 1.2 %collective-permute-start.8 = (f32[2,768]{1,0:T(2,128)S(1)}, f32[2,768]{1,0:T(2,128)S(1)}, u32[]{:S(2)}, u32[]{:S(2)}) collective-permute-start(f32[2,768]{1,0:T(2,128)S(1)} %get-tuple-element.54), channel_id=1, source_target_pairs={{0,1},{1,0},{2,3},{3,2},{4,5},{5,4},{6,7},{7,6},{8,9},{9,8},{10,11... | collective-permute-start | bytes 18440 | tf_op jit(solution)/shard_map/ppermute | solution.py:373
  31.9 3.8 %collective-permute-start.9 = (f32[4,768]{1,0:T(4,128)S(1)}, f32[4,768]{1,0:T(4,128)S(1)}, u32[]{:S(2)}, u32[]{:S(2)}) collective-permute-start(f32[4,768]{1,0:T(4,128)S(1)} %pad_maximum_fusion.1.refs_0_), channel_id=1, source_target_pairs={{0,2},{1,3},{2,0},{3,1},{4,6},{5,7},{6,4},{7,5},{8,10},{9,11},{10,... | collective-permute-start | bytes 36872 | tf_op jit(solution)/shard_map/ppermute | solution.py:405
